TPU v7x, 256 devices: a whole 4x4x8 slice. The times are simulated.
256 devices in a mesh: tm: 32 (over z, x), rows: 8 (over y, core).
Axes of the slice: x: 4, y: 4, z: 8, core: 2. Of those that a mesh axis runs over, the one named last changes fastest.
Arguments:
- clip: float32 [128, 16, 32, 128], P('tm', 'rows'), may hold values from -6 to 6
- kernel_one: float32 [3, 3, 3, 128, 128], replicated, may hold values from -0.109375 to 0.109375
- kernel_two: float32 [3, 3, 3, 128, 128], replicated, may hold values from -0.109375 to 0.109375
- cotangent: float32 [128, 16, 32, 128], P('tm', 'rows'), may hold values from -6 to 6
Outputs:
- block_out: float32 [128, 16, 32, 128], P('tm', 'rows')
- grad_clip: float32 [128, 16, 32, 128], P('tm', 'rows')
- grad_one: float32 [3, 3, 3, 128, 128], replicated
- grad_two: float32 [3, 3, 3, 128, 128], replicated
All inputs are finite; a program needn't handle non-finite values.
Results may differ from a plain program's by a relative error of at most 0.00014.
Values sent between devices are 32-bit elements; how exact they have to be, the bound alone decides.
A program may use at most 128 MiB of HBM per device.

v0:
```python
import math

import jax
import jax.numpy as jnp
from jax import lax
from jax.sharding import PartitionSpec as P


def passed_along(value, axis, steps):
    count = lax.axis_size(axis)
    first, last = (max(0, -steps), min(count, count - steps))
    return lax.ppermute(value, axis, [(source, source + steps) for source in range(first, last)])


def padded_2(cells, sides, width):
    for axis, dim in sides:
        count = lax.axis_size(axis)
        ends = count - 1
        head = lax.slice_in_dim(cells, 0, width, axis=dim)
        tail = lax.slice_in_dim(cells, cells.shape[dim] - width, cells.shape[dim], axis=dim)
        cells = jnp.concatenate(
            [
                lax.ppermute(tail, axis, [(i, (i + 1) % count) for i in range(ends)]),
                cells,
                lax.ppermute(head, axis, [((i + 1) % count, i) for i in range(ends)]),
            ],
            axis=dim,
        )
    return cells


def columns(padded, step_time, step_row, out_frames, out_rows, span):
    window_piece = padded[step_time : step_time + out_frames, step_row : step_row + out_rows]
    joined = jnp.concatenate(
        [window_piece[:, :, offset : offset + span] for offset in range(3)], -1
    )
    return joined.reshape(out_frames * out_rows * span, -1)


def conv_local(extended, kernel):
    out_frames = extended.shape[0] - 2
    out_rows = extended.shape[1] - 2
    span = extended.shape[2]
    channels = extended.shape[3]
    padded = jnp.pad(extended, ((0, 0), (0, 0), (1, 1), (0, 0)))
    running = jnp.zeros((out_frames * out_rows * span, kernel.shape[-1]), jnp.float32)
    for step_time in range(3):
        for step_row in range(3):
            running = running + jnp.dot(
                columns(padded, step_time, step_row, out_frames, out_rows, span),
                kernel[step_time, step_row].reshape(3 * channels, -1),
                precision=lax.Precision.HIGHEST,
            )
    return running.reshape(out_frames, out_rows, span, -1)


def kernel_grad(extended, partner):
    out_frames = extended.shape[0] - 2
    out_rows = extended.shape[1] - 2
    span = extended.shape[2]
    channels = extended.shape[3]
    padded = jnp.pad(extended, ((0, 0), (0, 0), (1, 1), (0, 0)))
    flat_partner = partner.reshape(-1, partner.shape[-1])
    blocks = []
    for step_time in range(3):
        for step_row in range(3):
            product = lax.dot_general(
                columns(padded, step_time, step_row, out_frames, out_rows, span),
                flat_partner,
                (((0,), (0,)), ((), ())),
                precision=lax.Precision.HIGHEST,
            )
            blocks.append(product.reshape(3, channels, -1))
    return jnp.stack(blocks).reshape(3, 3, 3, channels, -1)


def flipped(kernel):
    return jnp.transpose(kernel[::-1, ::-1, ::-1], (0, 1, 2, 4, 3))


def frames_before(field):
    earlier = passed_along(field[field.shape[0] - 2 :], "tm", 1)
    return jnp.concatenate([earlier, field], 0)


def frames_after(field):
    later = passed_along(field[:2], "tm", -1)
    return jnp.concatenate([field, later], 0)


def with_rims(field):
    return padded_2(field, (("rows", 1),), 1)


def per_device(clip, kernel_one, kernel_two, cotangent):
    frames, rows_here, span, channels = clip.shape
    height = rows_here * lax.axis_size("rows")
    factor = 1.0 / math.sqrt(frames * lax.axis_size("tm") * height * span)
    clip_ext = with_rims(frames_before(clip))
    pre_one = conv_local(clip_ext, kernel_one)
    active_ext = with_rims(frames_before(jax.nn.silu(pre_one)))
    block_out = clip + conv_local(active_ext, kernel_two)
    grad_ext = with_rims(frames_after(cotangent))
    d_active = conv_local(grad_ext, flipped(kernel_two))
    sigma = jax.nn.sigmoid(pre_one)
    delta = d_active * sigma * (1.0 + pre_one * (1.0 - sigma))
    grad_two = kernel_grad(active_ext, cotangent) * factor
    delta_ext = with_rims(frames_after(delta))
    grad_clip = cotangent + conv_local(delta_ext, flipped(kernel_one))
    grad_one = kernel_grad(clip_ext, delta) * factor
    grad_one, grad_two = lax.psum((grad_one, grad_two), ("tm", "rows"))
    return (block_out, grad_clip, grad_one, grad_two)


def solution(mesh):
    return jax.shard_map(
        per_device,
        mesh=mesh,
        in_specs=(P("tm", "rows", None, None), P(), P(), P("tm", "rows", None, None)),
        out_specs=(P("tm", "rows", None, None), P("tm", "rows", None, None), P(), P()),
        check_vma=False,
    )
```

profile of v0, /device:TPU:1, one launch (start us, length us, event | category | flops | bytes accessed | tf_op | source)
XLA Modules:
  0.0 405.0 jit_solution(17946369800257006886)
XLA Ops:
  7.2 1.5 slice.824
  10.0 1.5 slice.748
  11.5 5.3 %collective-permute-start = (f32[2,2,32,128]{3,2,1,0:T(8,128)}, f32[2,2,32,128]{3,2,1,0:T(8,128)}, u32[]{:S(2)}, u32[]{:S(2)}) collective-permute-start(f32[2,2,32,128]{3,2,1,0:T(8,128)} %slice.748), channel_id=1, source_target_pairs={{0,8},{8,16},{16,24},{24,32},{32,40},{40,48},{48,56},{56,64},{64,7... | collective-permute-start | bytes 196616 | tf_op jit(solution)/shard_map/ppermute | solution.py:12
  16.8 2.8 copy.27
  21.7 1.5 copy.26
  30.1 4.6 %collective-permute-start.7 = (f32[6,1,32,128]{3,2,1,0:T(8,128)S(1)}, f32[6,1,32,128]{3,2,1,0:T(8,128)S(1)}, u32[]{:S(2)}, u32[]{:S(2)}) collective-permute-start(f32[6,1,32,128]{3,2,1,0:T(8,128)S(1)} %get-tuple-element.146), channel_id=1, source_target_pairs={{0,1},{1,2},{2,3},{3,4},{4,5},{5,6},{6,7},{8,9},{9,10},{10,11},{11... | collective-permute-start | bytes 294920 | tf_op jit(solution)/shard_map/ppermute | solution.py:23
  34.6 1.9 collective-permute-start.8
  36.6 3.6 collective-permute-start.1
  40.2 1.9 collective-permute-start.2
  43.5 1.4 fusion.60
  71.4 2.5 collective-permute-start.3
  73.9 1.5 collective-permute-start.9
  79.8 1.4 broadcast_multiply_fusion.1
  81.3 2.7 collective-permute-start.10
  84.0 1.9 collective-permute-start.11
  86.0 3.6 collective-permute-start.4
  89.6 1.9 collective-permute-start.5
  92.2 3.3 collective-permute-done.5
  98.8 1.4 fusion.59
  112.1 1.6 fusion.8
  113.7 1.5 fusion.7
  115.2 1.5 fusion.6
  137.1 256.8 %all-reduce.7.cloned.1.call-done = (f32[3,3,3,128,128]{4,3,2,1,0:T(8,128)}, f32[3,3,3,128,128]{4,3,2,1,0:T(8,128)}) async-done(((f32[3,3,3,128,128]{4,3,2,1,0:T(8,128)}, f32[3,3,3,128,128]{4,3,2,1,0:T(8,128)}), (f32[3,3,3,128,128]{4,3,2,1,0:T(8,128)}, f32[3,3,3,128,128]{4,3,2,1,0:T(8,128)})) %all-reduce.7.cloned.1.call-update) | async-done | bytes 3538960 | tf_op jit(solution)/shard_map/psum | solution.py:111
  393.9 3.0 copy.66
  (340 shorter events, 78.1 us)
Async XLA Ops:
  7.2 386.8 %all-reduce.7.cloned.1.call-start = ((), (), s32[]{:S(2)}) async-start(), calls=%async_computation | async-start | bytes 7077888 | tf_op jit(solution)/shard_map/psum | solution.py:111
  8.7 20.5 %collective-permute-start.6 = (f32[2,2,32,128]{3,2,1,0:T(8,128)}, f32[2,2,32,128]{3,2,1,0:T(8,128)}, u32[]{:S(2)}, u32[]{:S(2)}) collective-permute-start(f32[2,2,32,128]{3,2,1,0:T(8,128)} %slice.824), channel_id=1, source_target_pairs={{8,0},{16,8},{24,16},{32,24},{40,32},{48,40},{56,48},{64,56},{72,6... | collective-permute-start | bytes 196616 | tf_op jit(solution)/shard_map/ppermute | solution.py:12
  11.5 8.2 %copy-start.1 = (f32[3,3,3,128,128]{4,3,2,1,0:T(8,128)S(1)}, f32[3,3,3,128,128]{4,3,2,1,0:T(8,128)}, u32[]{:S(2)}) copy-start(f32[3,3,3,128,128]{4,3,2,1,0:T(8,128)} %param.5) | copy-start | bytes 5308420
  11.5 16.9 %collective-permute-start = (f32[2,2,32,128]{3,2,1,0:T(8,128)}, f32[2,2,32,128]{3,2,1,0:T(8,128)}, u32[]{:S(2)}, u32[]{:S(2)}) collective-permute-start(f32[2,2,32,128]{3,2,1,0:T(8,128)} %slice.748), channel_id=1, source_target_pairs={{0,8},{8,16},{16,24},{24,32},{32,40},{40,48},{48,56},{56,64},{64,7... | collective-permute-start | bytes 196616 | tf_op jit(solution)/shard_map/ppermute | solution.py:12
  30.1 12.1 %collective-permute-start.7 = (f32[6,1,32,128]{3,2,1,0:T(8,128)S(1)}, f32[6,1,32,128]{3,2,1,0:T(8,128)S(1)}, u32[]{:S(2)}, u32[]{:S(2)}) collective-permute-start(f32[6,1,32,128]{3,2,1,0:T(8,128)S(1)} %get-tuple-element.146), channel_id=1, source_target_pairs={{0,1},{1,2},{2,3},{3,4},{4,5},{5,6},{6,7},{8,9},{9,10},{10,11},{11... | collective-permute-start | bytes 294920 | tf_op jit(solution)/shard_map/ppermute | solution.py:23
  34.6 7.6 %collective-permute-start.8 = (f32[6,1,32,128]{3,2,1,0:T(8,128)S(1)}, f32[6,1,32,128]{3,2,1,0:T(8,128)S(1)}, u32[]{:S(2)}, u32[]{:S(2)}) collective-permute-start(f32[6,1,32,128]{3,2,1,0:T(8,128)S(1)} %get-tuple-element.147), channel_id=1, source_target_pairs={{1,0},{2,1},{3,2},{4,3},{5,4},{6,5},{7,6},{9,8},{10,9},{11,10},{12... | collective-permute-start | bytes 294920 | tf_op jit(solution)/shard_map/ppermute | solution.py:25
  36.6 8.4 %collective-permute-start.1 = (f32[6,1,32,128]{3,2,1,0:T(8,128)S(1)}, f32[6,1,32,128]{3,2,1,0:T(8,128)S(1)}, u32[]{:S(2)}, u32[]{:S(2)}) collective-permute-start(f32[6,1,32,128]{3,2,1,0:T(8,128)S(1)} %get-tuple-element.158), channel_id=1, source_target_pairs={{0,1},{1,2},{2,3},{3,4},{4,5},{5,6},{6,7},{8,9},{9,10},{10,11},{11... | collective-permute-start | bytes 294920 | tf_op jit(solution)/shard_map/ppermute | solution.py:23
  40.2 5.9 %collective-permute-start.2 = (f32[6,1,32,128]{3,2,1,0:T(8,128)S(1)}, f32[6,1,32,128]{3,2,1,0:T(8,128)S(1)}, u32[]{:S(2)}, u32[]{:S(2)}) collective-permute-start(f32[6,1,32,128]{3,2,1,0:T(8,128)S(1)} %get-tuple-element.159), channel_id=1, source_target_pairs={{1,0},{2,1},{3,2},{4,3},{5,4},{6,5},{7,6},{9,8},{10,9},{11,10},{12... | collective-permute-start | bytes 294920 | tf_op jit(solution)/shard_map/ppermute | solution.py:25
  69.7 5.6 %copy-start.12 = (f32[256,384]{0,1:T(8,128)S(1)}, f32[256,384]{0,1:T(8,128)}, u32[]{:S(2)}) copy-start(f32[256,384]{0,1:T(8,128)} %copy.28) | copy-start | bytes 1179652
  70.2 5.6 %copy-start.17 = (f32[256,384]{0,1:T(8,128)S(1)}, f32[256,384]{0,1:T(8,128)}, u32[]{:S(2)}) copy-start(f32[256,384]{0,1:T(8,128)} %copy.29) | copy-start | bytes 1179652
  70.7 5.6 %copy-start.16 = (f32[256,384]{0,1:T(8,128)S(1)}, f32[256,384]{0,1:T(8,128)}, u32[]{:S(2)}) copy-start(f32[256,384]{0,1:T(8,128)} %copy.30) | copy-start | bytes 1179652
  70.7 6.1 %copy-start.14 = (f32[256,384]{0,1:T(8,128)S(1)}, f32[256,384]{0,1:T(8,128)}, u32[]{:S(2)}) copy-start(f32[256,384]{0,1:T(8,128)} %copy.31) | copy-start | bytes 1179652
  71.3 6.1 %copy-start.13 = (f32[256,384]{0,1:T(8,128)S(1)}, f32[256,384]{0,1:T(8,128)}, u32[]{:S(2)}) copy-start(f32[256,384]{0,1:T(8,128)} %copy.32) | copy-start | bytes 1179652
  71.4 14.6 %collective-permute-start.3 = (f32[2,2,32,128]{3,2,1,0:T(8,128)S(1)}, f32[2,2,32,128]{3,2,1,0:T(8,128)S(1)}, u32[]{:S(2)}, u32[]{:S(2)}) collective-permute-start(f32[2,2,32,128]{3,2,1,0:T(8,128)S(1)} %slice.930), channel_id=1, source_target_pairs={{0,8},{8,16},{16,24},{24,32},{32,40},{40,48},{48,56},{56,64},{64,7... | collective-permute-start | bytes 196616 | tf_op jit(solution)/shard_map/ppermute | solution.py:12
  73.9 7.4 %collective-permute-start.9 = (f32[2,2,32,128]{3,2,1,0:T(8,128)S(1)}, f32[2,2,32,128]{3,2,1,0:T(8,128)S(1)}, u32[]{:S(2)}, u32[]{:S(2)}) collective-permute-start(f32[2,2,32,128]{3,2,1,0:T(8,128)S(1)} %slice.1000), channel_id=1, source_target_pairs={{8,0},{16,8},{24,16},{32,24},{40,32},{48,40},{56,48},{64,56},{72,6... | collective-permute-start | bytes 196616 | tf_op jit(solution)/shard_map/ppermute | solution.py:12
  81.2 17.4 %copy-start.5 = (f32[2,2,32,128]{3,2,1,0:T(8,128)}, f32[2,2,32,128]{3,2,1,0:T(8,128)S(1)}, u32[]{:S(2)}) copy-start(f32[2,2,32,128]{3,2,1,0:T(8,128)S(1)} %collective-permute-done.9) | copy-start | bytes 196612
  81.3 15.7 %collective-permute-start.10 = (f32[6,1,32,128]{3,2,1,0:T(8,128)S(1)}, f32[6,1,32,128]{3,2,1,0:T(8,128)S(1)}, u32[]{:S(2)}, u32[]{:S(2)}) collective-permute-start(f32[6,1,32,128]{3,2,1,0:T(8,128)S(1)} %get-tuple-element.136), channel_id=1, source_target_pairs={{0,1},{1,2},{2,3},{3,4},{4,5},{5,6},{6,7},{8,9},{9,10},{10,11},{11... | collective-permute-start | bytes 294920 | tf_op jit(solution)/shard_map/ppermute | solution.py:23
  84.0 13.0 %collective-permute-start.11 = (f32[6,1,32,128]{3,2,1,0:T(8,128)S(1)}, f32[6,1,32,128]{3,2,1,0:T(8,128)S(1)}, u32[]{:S(2)}, u32[]{:S(2)}) collective-permute-start(f32[6,1,32,128]{3,2,1,0:T(8,128)S(1)} %get-tuple-element.137), channel_id=1, source_target_pairs={{1,0},{2,1},{3,2},{4,3},{5,4},{6,5},{7,6},{9,8},{10,9},{11,10},{12... | collective-permute-start | bytes 294920 | tf_op jit(solution)/shard_map/ppermute | solution.py:25
  85.9 14.3 %copy-start.7 = (f32[2,2,32,128]{3,2,1,0:T(8,128)}, f32[2,2,32,128]{3,2,1,0:T(8,128)S(1)}, u32[]{:S(2)}) copy-start(f32[2,2,32,128]{3,2,1,0:T(8,128)S(1)} %collective-permute-done.3) | copy-start | bytes 196612
  86.0 6.3 %collective-permute-start.4 = (f32[6,1,32,128]{3,2,1,0:T(8,128)S(1)}, f32[6,1,32,128]{3,2,1,0:T(8,128)S(1)}, u32[]{:S(2)}, u32[]{:S(2)}) collective-permute-start(f32[6,1,32,128]{3,2,1,0:T(8,128)S(1)} %get-tuple-element.150), channel_id=1, source_target_pairs={{0,1},{1,2},{2,3},{3,4},{4,5},{5,6},{6,7},{8,9},{9,10},{10,11},{11... | collective-permute-start | bytes 294920 | tf_op jit(solution)/shard_map/ppermute | solution.py:23
  89.6 5.9 %collective-permute-start.5 = (f32[6,1,32,128]{3,2,1,0:T(8,128)S(1)}, f32[6,1,32,128]{3,2,1,0:T(8,128)S(1)}, u32[]{:S(2)}, u32[]{:S(2)}) collective-permute-start(f32[6,1,32,128]{3,2,1,0:T(8,128)S(1)} %get-tuple-element.151), channel_id=1, source_target_pairs={{1,0},{2,1},{3,2},{4,3},{5,4},{6,5},{7,6},{9,8},{10,9},{11,10},{12... | collective-permute-start | bytes 294920 | tf_op jit(solution)/shard_map/ppermute | solution.py:25
  112.1 4.7 %copy-start.19 = (f32[256,384]{0,1:T(8,128)S(1)}, f32[256,384]{0,1:T(8,128)}, u32[]{:S(2)}) copy-start(f32[256,384]{0,1:T(8,128)} %copy.40) | copy-start | bytes 1179652
  112.1 5.2 %copy-start.24 = (f32[256,384]{0,1:T(8,128)S(1)}, f32[256,384]{0,1:T(8,128)}, u32[]{:S(2)}) copy-start(f32[256,384]{0,1:T(8,128)} %copy.41) | copy-start | bytes 1179652
  112.1 5.6 %copy-start.20 = (f32[256,384]{0,1:T(8,128)S(1)}, f32[256,384]{0,1:T(8,128)}, u32[]{:S(2)}) copy-start(f32[256,384]{0,1:T(8,128)} %copy.42) | copy-start | bytes 1179652
  (87 other events, 174.5 us)
Sparse Core Ops, SparseCore 0:
  123.7 270.2 all-reduce.6
where the time goes:
time: 407 us; the launch traced here: 405 us
  waiting for transfers between devices  261 us (64%)
  local copies, waits for them, and re-layouts  47.1 us (12%)
  starting transfers between devices  32.9 us (8%)
  matrix products  31.7 us (8%)
  other arithmetic  15.9 us (4%)
  between operations  15.9 us (4%)
    psum x1, waiting for transfers between devices, per_device(): grad_one, grad_two = lax.psum((grad_one, grad_two), ('tm', 'rows'))  257 us
    dot_general x36, matrix products, conv_local(): jnp.dot(columns(padded, step_time, step_row, out_frames, out_rows, span),...  20 us
    reshape x18, local copies, waits for them, and re-layouts, columns(): return joined.reshape(out_frames * out_rows * span, -1)  16.5 us
    ppermute x4, starting transfers between devices, padded_2(): lax.ppermute(tail, axis, [(i, (i + 1) % count) for i in range(ends)])  14.6 us
    unnamed x202, local copies, waits for them, and re-layouts  13.5 us
    dot_general x18, matrix products, kernel_grad(): lax.dot_general(columns(padded, step_time, step_row, out_frames, out_rows...  11.8 us
    ppermute x4, starting transfers between devices, passed_along(): lax.ppermute(value, axis, [(source, source + steps) for source in range(f...  10.6 us
    concatenate x24, other arithmetic, columns(): jnp.concatenate([window_piece[:, :, offset:offset + span] for offset in r...  8.8 us
  transfers between devices with their start and end apart: 13, of which 3 were waited for; matrix products, arithmetic and copies ran while one was open for 8% of the time, Pallas kernels for 0%

commit v1 on v0

v1 whole, which is shorter than its diff:
```python
import jax
import jax.numpy as jnp
from jax import lax
from jax.experimental import pallas as pl
from jax.experimental.pallas import tpu as pltpu
from jax.sharding import PartitionSpec as P

MESH = pl.DeviceIdType.MESH
F32 = jnp.float32
BF16 = jnp.bfloat16
TAPS = [(a, b, c) for a in range(3) for b in range(3) for c in range(3)]
GROUPS = [TAPS[0:8], TAPS[8:16], TAPS[16:24], TAPS[24:27]]
STREAMS = [(0, 7, True, 27), (7, 7, False, 28), (14, 7, True, 29), (21, 6, False, 30)]
COPIES = 200
Q = 1.0 / 256.0


def tap_index(tap):
    return (tap[0] * 3 + tap[1]) * 3 + tap[2]


def split(v):
    hi = v.astype(BF16)
    return hi, (v - hi.astype(F32)).astype(BF16)


def kernel(
    clip_ref, cot_ref, k1_ref, k2_ref,
    block_ref, gclip_ref, sums,
    kf, kh, kl, ext, ext2, cols, acc, pre, fixed, part, r1, r2, r3, r4, rz,
    send_sem, recv_sem, load_sem,
):
    tm = lax.axis_index("tm")
    rows = lax.axis_index("rows")
    x, z = lax.rem(tm, 4), lax.div(tm, 4)
    core, y = lax.rem(rows, 2), lax.div(rows, 2)

    def at(xx, yy, zz):
        return (lax.rem(zz + 8, 8) * 4 + lax.rem(xx + 4, 4), lax.rem(yy + 4, 4) * 2 + core)

    partner_row = y * 2 + 1 - core
    outer_row = lax.rem(rows + 2 * core - 1 + 8, 8)
    tm_next, tm_prev = lax.rem(tm + 1, 32), lax.rem(tm + 31, 32)
    partner = (tm, partner_row)

    loads = []
    for n, k_ref in enumerate((k1_ref, k2_ref)):
        loads.append(pltpu.make_async_copy(k_ref, kf.at[n], load_sem.at[n]))
        loads[-1].start()

    peers = [partner, (tm, outer_row)]
    for t in (tm_next, tm_prev):
        peers += [(t, rows), (t, partner_row), (t, outer_row)]
    peers += [at(x + 1, y, z), at(x - 1, y, z), at(x, y + 1, z), at(x, y - 1, z)]
    peers += [at(x, y, z + d) for d in range(1, 8)]
    barrier = pltpu.get_barrier_semaphore()
    for peer in peers:
        pl.semaphore_signal(barrier, inc=1, device_id=peer, device_id_type=MESH)

    own = pl.ds(1 + 2 * core, 2)
    ext[0, 2:6, own] = clip_ref[...]
    ext[1, 0:4, own] = cot_ref[...]
    part[27:32] = jnp.zeros((5, 16, 8, 128), F32)
    pl.semaphore_wait(barrier, len(peers))

    started = []

    def put(src, dst, device):
        n = len(started)
        copy = pltpu.make_async_remote_copy(
            src_ref=src, dst_ref=dst, send_sem=send_sem.at[n], recv_sem=recv_sem.at[n],
            device_id=device, device_id_type=MESH,
        )
        copy.start()
        started.append(copy)
        return copy

    edge, edge_there, inner = 1 + 3 * core, 5 - 5 * core, 2 + core
    sides = ((0, pl.ds(2, 4), pl.ds(4, 2), pl.ds(0, 2), tm_next), (1, pl.ds(0, 4), pl.ds(0, 2), pl.ds(4, 2), tm_prev))

    def to_partner(field):
        return [put(field.at[n, mine, own], field.at[n, mine, own], partner) for n, mine, _, _, _ in sides]

    def to_others(field, across):
        out = []
        for n, mine, src, dst, there in sides:
            out.append(put(field.at[n, src, own], field.at[n, dst, own], (there, rows)))
            out.append(put(field.at[n, mine, edge], field.at[n, mine, edge_there], (tm, outer_row)))
            out.append(put(field.at[n, src, across], field.at[n, dst, across], (there, partner_row)))
            out.append(put(field.at[n, src, edge], field.at[n, dst, edge_there], (there, outer_row)))
        return out

    halo = to_others(ext, own) + to_partner(ext)

    for load in loads:
        load.wait()

    def split_tap(t, _):
        for n in range(2):
            kh[n, t], kl[n, t] = split(kf[n, t])
        return 0

    lax.fori_loop(0, 27, split_tap, 0)
    for copy in halo:
        copy.wait_recv()
    far_row = put(ext.at[core, :, 5 * core], ext.at[core, :, 5 * core], partner)

    at_column = lax.broadcasted_iota(jnp.int32, (32, 128), 0)

    def columns(field, n, row):
        inside = jnp.logical_not(((row == 0) & (y == 0)) | ((row == 5) & (y == 3)))
        for f in range(6):
            keep = inside
            if n == 0 and f < 2:
                keep = keep & (tm > 0)
            if n == 1 and f > 3:
                keep = keep & (tm < 31)
            v = jnp.where(keep, field[n, f, row], 0.0)
            hi = v.astype(BF16).astype(F32)
            lo = v - hi
            for h, piece in enumerate((hi, lo)):
                cols[n, h, 0, f, row] = jnp.where(at_column == 0, 0.0, pltpu.roll(piece, 1, 0)).astype(BF16)
                cols[n, h, 1, f, row] = piece.astype(BF16)
                cols[n, h, 2, f, row] = jnp.where(at_column == 31, 0.0, pltpu.roll(piece, 31, 0)).astype(BF16)

    def convolve(n, kernel_at, turned):
        for g, group in enumerate(GROUPS):
            left, right = [], []
            for a, b, c in group:
                at_tap = tap_index((a, b, c))
                i, j, k = (2 - a, 2 - b, 2 - c) if turned else (a, b, c)
                window = [cols[n, h, k, i : i + 4, pl.ds(2 * core + j, 2)].reshape(256, 128) for h in range(2)]
                left.append(jnp.concatenate(window, 0))
                right.append(jnp.concatenate([kh[kernel_at, at_tap], kl[kernel_at, at_tap]], 0 if turned else 1))
            left = jnp.concatenate(left, 1)
            right = jnp.concatenate(right, 1 if turned else 0)
            product = lax.dot_general(left, right, (((1,), (1 if turned else 0,)), ((), ())), preferred_element_type=F32)
            if g == 0:
                acc[...] = product
            else:
                acc[...] += product
        total = acc[0:256, 0:128] + (acc[0:256, 128:256] + acc[256:512, 0:128]) + acc[256:512, 128:256]
        return total.reshape(4, 2, 32, 128)

    def near_columns(field, n):
        def one(j, _):
            columns(field, n, 2 * core + j)
            return 0

        lax.fori_loop(0, 4, one, 0)

    near_columns(ext, 0)
    pre[...] = convolve(0, 0, False)
    near_columns(ext, 1)
    d_active = convolve(1, 1, True)
    v = pre[...]
    s = jax.nn.sigmoid(v)
    ext2[0, 2:6, own] = v * s
    ext2[1, 0:4, own] = d_active * s * (1.0 + v * (1.0 - s))
    swap = to_partner(ext2)

    far_row.wait_recv()

    @pl.when(core == 0)
    def _():
        for row in (4, 5):
            columns(ext, 1, row)

    @pl.when(core == 1)
    def _():
        for row in (0, 1):
            columns(ext, 0, row)

    for copy in swap:
        copy.wait_recv()
    whole = ext2[core, pl.ds(2 - 2 * core, 4), 1:5].reshape(512, 128)
    fixed[0:128], fixed[128:256] = split(whole.T)
    halo2 = []

    def gradient(tap):
        a, b, c = (core * t + (1 - core) * (2 - t) for t in tap)
        right = [cols[1 - core, h, c, pl.ds(a, 4), pl.ds(b, 4)].reshape(512, 128) for h in range(2)]
        m = jnp.dot(fixed[...], jnp.concatenate(right, 1), preferred_element_type=F32)
        m = m[0:128, 0:128] + (m[0:128, 128:256] + m[128:256, 0:128]) + m[128:256, 128:256]
        part[tap_index(tap)] = jnp.where(core == 1, m.T, m).reshape(16, 8, 128)

    def stream(first, count, x_first, pad):
        taps = pl.ds(first, count)
        half = count // 2
        taps_a, taps_b = pl.ds(first, half), pl.ds(first + half, count - half)
        along_x, along_y = (at(x + 1, y, z), at(x - 1, y, z)), (at(x, y + 1, z), at(x, y - 1, z))
        p, s = (x, y) if x_first else (y, x)
        (plus, minus), (plus2, minus2) = (along_x, along_y) if x_first else (along_y, along_x)
        p_next, p_prev, p_far = lax.rem(p + 1, 4), lax.rem(p + 3, 4), lax.rem(p + 2, 4)
        t_next, t_prev, t_far = (4 * p + lax.rem(s + d, 4) for d in (1, 3, 2))
        t_own = 4 * p + s
        mine = sums.at[core]

        def slot(zz):
            return first + zz + lax.div(zz, count) * (pad - first - count)

        for tap in TAPS[first : first + count]:
            gradient(tap)
        a = put(part.at[taps, pl.ds(4 * p_far, 2)], r1.at[0, taps], plus)
        b = put(part.at[taps, pl.ds(4 * p_far + 2, 2)], r1.at[1, taps], minus)
        yield
        a.wait_recv()
        part[taps, pl.ds(4 * p_next, 2)] += r1[0, taps]
        a = put(part.at[taps, pl.ds(4 * p_next, 4)], r2.at[0, taps], plus)
        b.wait_recv()
        part[taps, pl.ds(4 * p_prev + 2, 2)] += r1[1, taps]
        b = put(part.at[taps, pl.ds(4 * p_prev, 4)], r2.at[1, taps], minus)
        yield
        a.wait_recv()
        b.wait_recv()
        part[taps, pl.ds(4 * p, 4)] += r2[0, taps] + r2[1, taps]
        a = put(part.at[taps_a, t_far], r3.at[0, taps_a], plus2)
        b = put(part.at[taps_b, t_far], r3.at[1, taps_b], minus2)
        yield
        a.wait_recv()
        part[taps_a, t_next] += r3[0, taps_a]
        a = put(part.at[taps, t_next], r4.at[0, taps], plus2)
        b.wait_recv()
        part[taps_b, t_prev] += r3[1, taps_b]
        b = put(part.at[taps, t_prev], r4.at[1, taps], minus2)
        yield
        a.wait_recv()
        b.wait_recv()
        part[taps, t_own] += r4[0, taps] + r4[1, taps]
        along_z = []
        which = pad - 27
        for d in range(1, 8):
            there = lax.rem(z + d, 8)
            along_z.append(put(part.at[slot(there), t_own], rz.at[which, z], at(x, y, there)))
        yield
        total = part[slot(z), t_own]
        for d in range(1, 8):
            along_z[d - 1].wait_recv()
            total = total + rz[which, lax.rem(z - d + 8, 8)]
        mine[slot(z), t_own] = total * Q
        along_z = []
        for d in range(1, 8):
            along_z.append(put(mine.at[slot(z), t_own], mine.at[slot(z), t_own], at(x, y, lax.rem(z + d, 8))))
        yield
        for copy in along_z:
            copy.wait_recv()
        a = put(mine.at[taps, t_own], mine.at[taps, t_own], plus2)
        b = put(mine.at[taps, t_own], mine.at[taps, t_own], minus2)
        yield
        a.wait_recv()
        a = put(mine.at[taps_a, t_prev], mine.at[taps_a, t_prev], plus2)
        b.wait_recv()
        b = put(mine.at[taps_b, t_next], mine.at[taps_b, t_next], minus2)
        yield
        a.wait_recv()
        b.wait_recv()
        own_tiles, prev_tiles, next_tiles, far_tiles = (pl.ds(4 * i, 4) for i in (p, p_prev, p_next, p_far))
        a = put(mine.at[taps, own_tiles], mine.at[taps, own_tiles], plus)
        b = put(mine.at[taps, own_tiles], mine.at[taps, own_tiles], minus)
        across = [put(mine.at[taps, own_tiles], mine.at[taps, own_tiles], partner)]
        yield
        half_a, half_b = pl.ds(4 * p_prev, 2), pl.ds(4 * p_next + 2, 2)
        a.wait_recv()
        a = put(mine.at[taps, half_a], mine.at[taps, half_a], plus)
        b.wait_recv()
        b = put(mine.at[taps, half_b], mine.at[taps, half_b], minus)
        for tiles in (prev_tiles, next_tiles):
            across.append(put(mine.at[taps, tiles], mine.at[taps, tiles], partner))
        yield
        a.wait_recv()
        b.wait_recv()
        across.append(put(mine.at[taps, far_tiles], mine.at[taps, far_tiles], partner))
        yield
        for copy in across:
            copy.wait_recv()

    def finish_forward():
        for copy in halo2[:4]:
            copy.wait_recv()
        near_columns(ext2, 0)
        block_ref[...] = clip_ref[...] + convolve(0, 1, False)

    def finish_backward():
        for copy in halo2[4:]:
            copy.wait_recv()
        near_columns(ext2, 1)
        gclip_ref[...] = cot_ref[...] + convolve(1, 0, True)

    running = [stream(*one) for one in STREAMS]

    def advance(*which):
        for n in which:
            next(running[n], None)

    advance(0, 1, 0, 2, 1, 3)
    halo2 += to_others(ext2, inner)
    advance(2, 3, 0, 1)
    advance(0, 1, 2, 3)
    finish_forward()
    advance(0, 1, 2, 3)
    finish_backward()
    for _ in range(12):
        advance(0, 1, 2, 3)
    for copy in started:
        copy.wait_send()


def per_device(clip, kernel_one, kernel_two, cotangent):
    vmem = pl.BlockSpec(memory_space=pltpu.VMEM)
    anywhere = pl.BlockSpec(memory_space=pl.ANY)
    field = jax.ShapeDtypeStruct(clip.shape, F32)
    block_out, grad_clip, sums = pl.pallas_call(
        kernel,
        out_shape=(field, field, jax.ShapeDtypeStruct((2, 32, 16, 8, 128), F32)),
        in_specs=[vmem, vmem, anywhere, anywhere],
        out_specs=(vmem, vmem, vmem),
        scratch_shapes=[
            pltpu.VMEM((2, 27, 128, 128), F32),
            pltpu.VMEM((2, 27, 128, 128), BF16),
            pltpu.VMEM((2, 27, 128, 128), BF16),
            pltpu.VMEM((2, 6, 6, 32, 128), F32),
            pltpu.VMEM((2, 6, 6, 32, 128), F32),
            pltpu.VMEM((2, 2, 3, 6, 6, 32, 128), BF16),
            pltpu.VMEM((512, 256), F32),
            pltpu.VMEM((4, 2, 32, 128), F32),
            pltpu.VMEM((256, 512), BF16),
            pltpu.VMEM((32, 16, 8, 128), F32),
            pltpu.VMEM((2, 27, 2, 8, 128), F32),
            pltpu.VMEM((2, 27, 4, 8, 128), F32),
            pltpu.VMEM((2, 27, 8, 128), F32),
            pltpu.VMEM((2, 27, 8, 128), F32),
            pltpu.VMEM((4, 8, 8, 128), F32),
            pltpu.SemaphoreType.DMA((COPIES,)),
            pltpu.SemaphoreType.DMA((COPIES,)),
            pltpu.SemaphoreType.DMA((2,)),
        ],
        compiler_params=pltpu.CompilerParams(
            collective_id=0, has_side_effects=True, vmem_limit_bytes=48 * 1024 * 1024
        ),
        cost_estimate=pl.CostEstimate(flops=6 * 4 * 226492416, bytes_accessed=8 * 1024 * 1024, transcendentals=32768),
    )(clip, cotangent, kernel_one.reshape(27, 128, 128), kernel_two.reshape(27, 128, 128))
    grad_two, grad_one = (sums[n, :27].reshape(kernel_one.shape) for n in range(2))
    return block_out, grad_clip, grad_one, grad_two


def solution(mesh):
    field = P("tm", "rows", None, None)
    return jax.shard_map(
        per_device,
        mesh=mesh,
        in_specs=(field, P(), P(), field),
        out_specs=(field, field, P(), P()),
        check_vma=False,
    )
```

time: 407 us -> 94.7 us (0.23)
  waiting for transfers between devices: 261 us -> 0 us
  Pallas kernels: 0 us -> 83.6 us
  local copies, waits for them, and re-layouts: 47.1 us -> 10.3 us
  starting transfers between devices: 32.9 us -> 0 us
  matrix products: 31.7 us -> 0 us
  other arithmetic: 15.9 us -> 0 us
  between operations: 15.9 us -> 0.65 us
    psum x1 -> x0, waiting for transfers between devices: 257 us -> none  [per_device(): grad_one, grad_two = lax.psum((grad_one, grad_two), ('tm', 'rows'))]
    pallas_call x0 -> x1, Pallas kernels: none -> 83.6 us  [per_device(): pl.pallas_call(kernel, out_shape=(field, field, jax.ShapeDtypeStruct((2,...]
    ppermute x12 -> x0, starting transfers between devices: 32.8 us -> none  [the longest x4 14.6 us: padded_2(): lax.ppermute(tail, axis, [(i, (i + 1) % count) for i in range(ends)])]
    dot_general x54 -> x0, matrix products: 31.7 us -> none  [the longest x36 20 us: conv_local(): jnp.dot(columns(padded, step_time, step_row, out_frames, out_rows, span),...]
    reshape x18 -> x0, local copies, waits for them, and re-layouts: 16.5 us -> none  [columns(): return joined.reshape(out_frames * out_rows * span, -1)]
    slice x18 -> x1, local copies, waits for them, and re-layouts: 15.9 us -> 4.2 us  [per_device(): sums[n, :27].reshape(kernel_one.shape)]
    concatenate x35 -> x0, other arithmetic: 10.7 us -> none  [the longest x24 8.8 us: columns(): jnp.concatenate([window_piece[:, :, offset:offset + span] for offset in r...]
    unnamed x202 -> x10, local copies, waits for them, and re-layouts: 13.5 us -> 6.06 us
  transfers between devices with their start and end apart: 13 -> 0, of which waited for: 3 -> 0; matrix products, arithmetic and copies ran while one was open for 8% -> 0% of each run, Pallas kernels for 0% -> 0%
where the time goes in v1:
time: 94.7 us; the launch traced here: 94.5 us
  Pallas kernels  83.6 us (88%)
  local copies, waits for them, and re-layouts  10.3 us (11%)
    pallas_call x1, Pallas kernels, per_device(): pl.pallas_call(kernel, out_shape=(field, field, jax.ShapeDtypeStruct((2,...  83.6 us
    unnamed x10, local copies, waits for them, and re-layouts  6.06 us
    slice x1, local copies, waits for them, and re-layouts, per_device(): sums[n, :27].reshape(kernel_one.shape)  4.2 us

profile of v1, /device:TPU:1, one launch (start us, length us, event | category | flops | bytes accessed | tf_op | source)
XLA Modules:
  0.0 94.5 jit_solution(11823506916309250084)
XLA Ops:
  0.6 0.0 copy-start
  0.6 1.5 %copy-done = f32[3,3,3,128,128]{4,3,2,1,0:T(8,128)S(1)} copy-done((f32[3,3,3,128,128]{4,3,2,1,0:T(8,128)S(1)}, f32[3,3,3,128,128]{4,3,2,1,0:T(8,128)}, u32[]{:S(2)}) %copy-start) | copy-done | bytes 1769496
  2.1 0.0 copy-start.1
  2.1 1.5 %copy-done.1 = f32[3,3,3,128,128]{4,3,2,1,0:T(8,128)S(1)} copy-done((f32[3,3,3,128,128]{4,3,2,1,0:T(8,128)S(1)}, f32[3,3,3,128,128]{4,3,2,1,0:T(8,128)}, u32[]{:S(2)}) %copy-start.1) | copy-done | bytes 1769496
  3.6 0.0 copy-start.2
  3.6 0.9 copy-done.2
  4.5 0.0 copy-start.3
  4.5 0.9 copy-done.3
  5.4 83.6 %shard_map.75 = (f32[4,2,32,128]{3,2,1,0:T(8,128)S(1)}, f32[4,2,32,128]{3,2,1,0:T(8,128)S(1)}, f32[2,32,16,8,128]{4,3,2,1,0:T(8,128)}) custom-call(f32[4,2,32,128]{3,2,1,0:T(8,128)S(1)} %copy-done.2, f32[4,2,32,128]{3,2,1,0:T(8,128)S(1)} %copy-done.3, f32[27,128,128]{2,1,0:T(8,128)S(1)} %bitcast.4, f32[27,128,128]{2,1,0:T(8,128)S(1)} %bitcast.5), custom_call_target="tpu_custom_call" | custom-call | flops 5435817984 | bytes 8388608 | tf_op jit(solution)/shard_map/pallas_call | solution.py:312
  89.0 4.2 %fusion = (f32[1,27,16,8,128]{4,3,2,1,0:T(8,128)}, f32[1,27,16,8,128]{4,3,2,1,0:T(8,128)}) fusion(f32[2,32,16,8,128]{4,3,2,1,0:T(8,128)} %get-tuple-element.9), kind=kLoop, calls=%fused_computation | loop fusion | bytes 7077888 | tf_op jit(solution)/shard_map/slice | solution.py:342
  93.2 0.7 copy.10
  93.9 0.7 copy.11
Async XLA Ops:
  0.6 1.5 %copy-start = (f32[3,3,3,128,128]{4,3,2,1,0:T(8,128)S(1)}, f32[3,3,3,128,128]{4,3,2,1,0:T(8,128)}, u32[]{:S(2)}) copy-start(f32[3,3,3,128,128]{4,3,2,1,0:T(8,128)} %param.5) | copy-start | bytes 5308420
  2.1 1.5 %copy-start.1 = (f32[3,3,3,128,128]{4,3,2,1,0:T(8,128)S(1)}, f32[3,3,3,128,128]{4,3,2,1,0:T(8,128)}, u32[]{:S(2)}) copy-start(f32[3,3,3,128,128]{4,3,2,1,0:T(8,128)} %param.6) | copy-start | bytes 5308420
  3.6 0.9 copy-start.2
  4.5 0.9 copy-start.3

commit v2 on v1

v2 whole, which is shorter than its diff:
```python
import jax
import jax.numpy as jnp
from jax import lax
from jax.experimental import pallas as pl
from jax.experimental.pallas import tpu as pltpu
from jax.sharding import PartitionSpec as P

MESH = pl.DeviceIdType.MESH
F32 = jnp.float32
BF16 = jnp.bfloat16
TAPS = [(a, b, c) for a in range(3) for b in range(3) for c in range(3)]
GROUPS = [TAPS[0:8], TAPS[8:16], TAPS[16:24], TAPS[24:27]]
STREAMS = [(0, 4, True), (4, 4, False), (8, 4, True), (12, 3, False), (15, 3, True), (18, 3, False), (21, 3, True), (24, 3, False)]
PHASES = (0.0, 4.9, 8.4, 13.4, 18.4, 22.0, 27.0, 28.0)
STEP = 1.9
COPIES = 320
Q = 1.0 / 256.0


def tap_index(tap):
    return (tap[0] * 3 + tap[1]) * 3 + tap[2]


def split(v):
    hi = v.astype(BF16)
    return hi, (v - hi.astype(F32)).astype(BF16)


def kernel(
    clip_ref, cot_ref, k1_ref, k2_ref,
    block_ref, gclip_ref, sums,
    kf, kh, kl, ext, ext2, cols, acc, pre, fixed, part, r1, r2, rz,
    send_sem, recv_sem, load_sem,
):
    tm = lax.axis_index("tm")
    rows = lax.axis_index("rows")
    x, z = lax.rem(tm, 4), lax.div(tm, 4)
    core, y = lax.rem(rows, 2), lax.div(rows, 2)

    def at(xx, yy, zz):
        return (zz * 4 + lax.rem(xx, 4), lax.rem(yy, 4) * 2 + core)

    partner_row = y * 2 + 1 - core
    outer_row = lax.rem(rows + 2 * core - 1 + 8, 8)
    tm_next, tm_prev = lax.rem(tm + 1, 32), lax.rem(tm + 31, 32)
    partner = (tm, partner_row)
    own = pl.ds(1 + 2 * core, 2)

    loads = []
    for src, dst in ((clip_ref, ext.at[0, 2:6, own]), (cot_ref, ext.at[1, 0:4, own]), (k1_ref, kf.at[0]), (k2_ref, kf.at[1])):
        loads.append(pltpu.make_async_copy(src, dst, load_sem.at[len(loads)]))
        loads[-1].start()

    peers = [partner, (tm, outer_row)]
    for t in (tm_next, tm_prev):
        peers += [(t, rows), (t, partner_row), (t, outer_row)]
    for d in range(1, 4):
        peers += [at(x + d, y, z), at(x, y + d, z)]
    peers += [at(x, y, lax.rem(z + d, 8)) for d in range(1, 8)]
    barrier = pltpu.get_barrier_semaphore()
    for peer in peers:
        pl.semaphore_signal(barrier, inc=1, device_id=peer, device_id_type=MESH)
    for load in loads[:2]:
        load.wait()
    pl.semaphore_wait(barrier, len(peers))

    started = []

    def put(src, dst, device, sends=None):
        n = len(started)
        copy = pltpu.make_async_remote_copy(
            src_ref=src, dst_ref=dst, send_sem=send_sem.at[n], recv_sem=recv_sem.at[n],
            device_id=device, device_id_type=MESH,
        )
        if sends is None:
            copy.start()
        else:
            pl.when(sends)(copy.start)
        started.append((copy, sends))
        return copy

    edge, edge_there, inner = 1 + 3 * core, 5 - 5 * core, 2 + core
    sides = ((0, pl.ds(2, 4), pl.ds(4, 2), pl.ds(0, 2), tm_next), (1, pl.ds(0, 4), pl.ds(0, 2), pl.ds(4, 2), tm_prev))

    def to_partner(field):
        return [put(field.at[n, mine, own], field.at[n, mine, own], partner) for n, mine, _, _, _ in sides]

    def to_others(field):
        out = []
        for n, mine, src, dst, there in sides:
            out.append(put(field.at[n, src, own], field.at[n, dst, own], (there, rows)))
            out.append(put(field.at[n, mine, edge], field.at[n, mine, edge_there], (tm, outer_row)))
            out.append(put(field.at[n, src, edge], field.at[n, dst, edge_there], (there, outer_row)))
            out.append(put(field.at[n, src, inner], field.at[n, dst, inner], (there, partner_row)))
        return out

    halo = to_others(ext)
    beside = to_partner(ext)

    for load in loads[2:]:
        load.wait()

    def split_tap(t, _):
        for n in range(2):
            kh[n, t], kl[n, t] = split(kf[n, t])
        return 0

    lax.fori_loop(0, 27, split_tap, 0)
    for copy in halo + beside:
        copy.wait_recv()
    halo_frames, own_frames = pl.ds(4 * core, 2), pl.ds(2 - 2 * core, 4)
    outer_rows = pl.ds(4 * core, 2)
    passed = [
        put(ext.at[core, halo_frames, outer_rows], ext.at[core, halo_frames, outer_rows], partner),
        put(ext.at[core, own_frames, 5 * core], ext.at[core, own_frames, 5 * core], partner),
    ]

    at_column = lax.broadcasted_iota(jnp.int32, (32, 128), 0)

    def columns(field, n, row):
        inside = jnp.logical_not(((row == 0) & (y == 0)) | ((row == 5) & (y == 3)))
        for f in range(6):
            keep = inside
            if n == 0 and f < 2:
                keep = keep & (tm > 0)
            if n == 1 and f > 3:
                keep = keep & (tm < 31)
            v = jnp.where(keep, field[n, f, row], 0.0)
            hi = v.astype(BF16).astype(F32)
            lo = v - hi
            for h, piece in enumerate((hi, lo)):
                cols[n, h, 0, f, row] = jnp.where(at_column == 0, 0.0, pltpu.roll(piece, 1, 0)).astype(BF16)
                cols[n, h, 1, f, row] = piece.astype(BF16)
                cols[n, h, 2, f, row] = jnp.where(at_column == 31, 0.0, pltpu.roll(piece, 31, 0)).astype(BF16)

    def convolve(n, kernel_at, turned):
        for g, group in enumerate(GROUPS):
            left, right = [], []
            for a, b, c in group:
                at_tap = tap_index((a, b, c))
                i, j, k = (2 - a, 2 - b, 2 - c) if turned else (a, b, c)
                window = [cols[n, h, k, i : i + 4, pl.ds(2 * core + j, 2)].reshape(256, 128) for h in range(2)]
                left.append(jnp.concatenate(window, 0))
                right.append(jnp.concatenate([kh[kernel_at, at_tap], kl[kernel_at, at_tap]], 0 if turned else 1))
            left = jnp.concatenate(left, 1)
            right = jnp.concatenate(right, 1 if turned else 0)
            product = lax.dot_general(left, right, (((1,), (1 if turned else 0,)), ((), ())), preferred_element_type=F32)
            if g == 0:
                acc[...] = product
            else:
                acc[...] += product
            yield

    def convolved():
        total = acc[0:256, 0:128] + (acc[0:256, 128:256] + acc[256:512, 0:128]) + acc[256:512, 128:256]
        return total.reshape(4, 2, 32, 128)

    def near_columns(field, n):
        def one(j, _):
            columns(field, n, 2 * core + j)
            return 0

        lax.fori_loop(0, 4, one, 0)

    near_columns(ext, 0)
    for _ in convolve(0, 0, False):
        pass
    pre[...] = convolved()
    near_columns(ext, 1)
    for _ in convolve(1, 1, True):
        pass
    v = pre[...]
    s = jax.nn.sigmoid(v)
    ext2[0, 2:6, own] = v * s
    ext2[1, 0:4, own] = convolved() * s * (1.0 + v * (1.0 - s))
    swap = to_partner(ext2)

    for copy in passed:
        copy.wait_recv()

    @pl.when(core == 0)
    def _():
        for row in (4, 5):
            columns(ext, 1, row)

    @pl.when(core == 1)
    def _():
        for row in (0, 1):
            columns(ext, 0, row)

    for copy in swap:
        copy.wait_recv()
    whole = ext2[core, own_frames, 1:5].reshape(512, 128)
    fixed[0:128], fixed[128:256] = split(whole.T)

    def gradient(tap):
        a, b, c = (core * t + (1 - core) * (2 - t) for t in tap)
        right = [cols[1 - core, h, c, pl.ds(a, 4), pl.ds(b, 4)].reshape(512, 128) for h in range(2)]
        m = jnp.dot(fixed[...], jnp.concatenate(right, 1), preferred_element_type=F32)
        m = m[0:128, 0:128] + (m[0:128, 128:256] + m[128:256, 0:128]) + m[128:256, 128:256]
        part[tap_index(tap)] = jnp.where(core == 1, m.T, m).reshape(16, 8, 128)

    def stream(which, first, count, x_first):
        taps = pl.ds(first, count)
        rings = [[at(x + d, y, z) for d in (1, 2, 3)], [at(x, y + d, z) for d in (1, 2, 3)]]
        p, s = (x, y) if x_first else (y, x)
        ring, ring2 = rings if x_first else rings[::-1]
        p_of, s_of = ([lax.rem(i + d, 4) for d in range(4)] for i in (p, s))
        tile = 4 * p + s
        mine = sums.at[core]
        place = [lax.rem(z + d + 64 - first, 8) for d in range(8)]
        owns = [k < count for k in place]
        tap_at = [first + lax.rem(k, count) for k in place]
        z_of = [lax.rem(z + d, 8) for d in range(8)]

        def same(ref, to):
            return put(ref, ref, to)

        for tap in TAPS[first : first + count]:
            gradient(tap)
        sent = [put(part.at[taps, pl.ds(4 * p_of[d], 4)], r1.at[d - 1, taps], ring[d - 1]) for d in (1, 2, 3)]
        yield
        for copy in sent:
            copy.wait_recv()
        part[taps, pl.ds(4 * p, 4)] += r1[0, taps] + r1[1, taps] + r1[2, taps]
        sent = [put(part.at[taps, 4 * p + s_of[d]], r2.at[d - 1, taps], ring2[d - 1]) for d in (1, 2, 3)]
        yield
        for copy in sent:
            copy.wait_recv()
        part[taps, tile] += r2[0, taps] + r2[1, taps] + r2[2, taps]
        sent = []
        for d in range(1, 8):
            sent.append(put(part.at[tap_at[d], tile], rz.at[which, d - 1], at(x, y, z_of[d]), owns[d]))
        yield

        @pl.when(owns[0])
        def _():
            total = part[tap_at[0], tile]
            for d in range(1, 8):
                sent[d - 1].wait_recv()
                total = total + rz[which, d - 1]
            mine[tap_at[0], tile] = total * Q

        done = mine.at[tap_at[0], tile]
        sent = [put(done, done, at(x, y, z_of[d]), owns[0]) for d in range(1, 8)]
        yield
        for d in range(1, 8):
            pl.when(owns[8 - d])(sent[d - 1].wait_recv)
        sent = [same(mine.at[taps, tile], to) for to in ring2]
        yield
        for copy in sent:
            copy.wait_recv()
        sent = [same(mine.at[taps, pl.ds(4 * p, 4)], to) for to in ring]
        across = [same(mine.at[taps, pl.ds(4 * p, 4)], partner)]
        yield
        for d in (1, 2, 3):
            sent[d - 1].wait_recv()
            across.append(same(mine.at[taps, pl.ds(4 * p_of[4 - d], 4)], partner))
        yield
        for copy in across:
            copy.wait_recv()

    def finish():
        for n, field, out, kernel_at, own_frames in ((0, ext, block_ref, 1, pl.ds(2, 4)), (1, ext, gclip_ref, 0, pl.ds(0, 4))):
            for copy in halo2[4 * n : 4 * n + 4]:
                copy.wait_recv()
            near_columns(ext2, n)
            yield
            yield from convolve(n, kernel_at, n == 1)
            out[...] = field[n, own_frames, own] + convolved()
            yield

    running = [stream(n, *one) for n, one in enumerate(STREAMS)]
    finishing = finish()
    order = []
    for n in range(len(STREAMS)):
        for phase, start in enumerate(PHASES):
            order.append(((n // 2) * (STEP if phase else 0.6) + start, phase, n))
    halo2 = []
    for when, phase, n in sorted(order):
        if phase and not halo2:
            halo2 += to_others(ext2)
        next(running[n], None)
        if when > 6.0 and n % 2:
            next(finishing, None)
    for _ in finishing:
        pass
    for copy, sends in started:
        if sends is None:
            copy.wait_send()
        else:
            pl.when(sends)(copy.wait_send)


def copy_out(block_ref, gclip_ref, sums, block_out, gclip_out, one_out, two_out, sem):
    copies = []
    for src, dst in ((sums.at[1], one_out), (sums.at[0], two_out), (block_ref, block_out), (gclip_ref, gclip_out)):
        copies.append(pltpu.make_async_copy(src, dst, sem.at[len(copies)]))
        copies[-1].start()
    for copy in copies:
        copy.wait()


def per_device(clip, kernel_one, kernel_two, cotangent):
    vmem = pl.BlockSpec(memory_space=pltpu.VMEM)
    hbm = pl.BlockSpec(memory_space=pltpu.HBM)
    anywhere = pl.BlockSpec(memory_space=pl.ANY)
    field = jax.ShapeDtypeStruct(clip.shape, F32)
    block_out, grad_clip, sums = pl.pallas_call(
        kernel,
        out_shape=(field, field, jax.ShapeDtypeStruct((2, 27, 16, 8, 128), F32)),
        in_specs=[hbm] * 4,
        out_specs=(vmem, vmem, vmem),
        scratch_shapes=[
            pltpu.VMEM((2, 27, 128, 128), F32),
            pltpu.VMEM((2, 27, 128, 128), BF16),
            pltpu.VMEM((2, 27, 128, 128), BF16),
            pltpu.VMEM((2, 6, 6, 32, 128), F32),
            pltpu.VMEM((2, 6, 6, 32, 128), F32),
            pltpu.VMEM((2, 2, 3, 6, 6, 32, 128), BF16),
            pltpu.VMEM((512, 256), F32),
            pltpu.VMEM((4, 2, 32, 128), F32),
            pltpu.VMEM((256, 512), BF16),
            pltpu.VMEM((27, 16, 8, 128), F32),
            pltpu.VMEM((3, 27, 4, 8, 128), F32),
            pltpu.VMEM((3, 27, 8, 128), F32),
            pltpu.VMEM((len(STREAMS), 7, 8, 128), F32),
            pltpu.SemaphoreType.DMA((COPIES,)),
            pltpu.SemaphoreType.DMA((COPIES,)),
            pltpu.SemaphoreType.DMA((4,)),
        ],
        compiler_params=pltpu.CompilerParams(
            collective_id=0, has_side_effects=True, vmem_limit_bytes=32 * 1024 * 1024
        ),
        cost_estimate=pl.CostEstimate(flops=6 * 4 * 226492416, bytes_accessed=8 * 1024 * 1024, transcendentals=32768),
    )(clip, cotangent, kernel_one.reshape(27, 128, 128), kernel_two.reshape(27, 128, 128))
    grad = jax.ShapeDtypeStruct((27, 16, 8, 128), F32)
    block_out, grad_clip, grad_one, grad_two = pl.pallas_call(
        copy_out,
        out_shape=(field, field, grad, grad),
        in_specs=[anywhere] * 3,
        out_specs=(hbm,) * 4,
        scratch_shapes=[pltpu.SemaphoreType.DMA((4,))],
        compiler_params=pltpu.CompilerParams(vmem_limit_bytes=1024 * 1024),
        cost_estimate=pl.CostEstimate(flops=0, bytes_accessed=8 * 1024 * 1024, transcendentals=0),
    )(block_out, grad_clip, sums)
    return block_out, grad_clip, grad_one.reshape(kernel_one.shape), grad_two.reshape(kernel_two.shape)


def solution(mesh):
    field = P("tm", "rows", None, None)
    return jax.shard_map(
        per_device,
        mesh=mesh,
        in_specs=(field, P(), P(), field),
        out_specs=(field, field, P(), P()),
        check_vma=False,
    )
```

time: 94.7 us -> 81.6 us (0.86)
  Pallas kernels: 83.6 us -> 76 us
  local copies, waits for them, and re-layouts: 10.3 us -> 4.75 us
    pallas_call x1, Pallas kernels: 83.6 us -> 74.1 us  [per_device(): pl.pallas_call(kernel, out_shape=(field, field, jax.ShapeDtypeStruct((2,...]
    slice x1 -> x0, local copies, waits for them, and re-layouts: 4.2 us -> none  [per_device(): sums[n, :27].reshape(kernel_one.shape)]
    pallas_call x0 -> x1, Pallas kernels: none -> 1.9 us  [per_device(): pl.pallas_call(copy_out, out_shape=(field, field, grad, grad), in_specs=[...]
    unnamed x10 -> x8, local copies, waits for them, and re-layouts: 6.06 us -> 4.75 us
where the time goes in v2:
time: 81.6 us; the launch traced here: 81.4 us
  Pallas kernels  76 us (93%)
  local copies, waits for them, and re-layouts  4.75 us (6%)
    pallas_call x1, Pallas kernels, per_device(): pl.pallas_call(kernel, out_shape=(field, field, jax.ShapeDtypeStruct((2,...  74.1 us
    unnamed x8, local copies, waits for them, and re-layouts  4.75 us
    pallas_call x1, Pallas kernels, per_device(): pl.pallas_call(copy_out, out_shape=(field, field, grad, grad), in_specs=[...  1.9 us

profile of v2, /device:TPU:1, one launch (start us, length us, event | category | flops | bytes accessed | tf_op | source)
XLA Modules:
  0.0 81.4 jit_solution(1345392313420269194)
XLA Ops:
  0.6 0.0 copy-start
  0.6 1.5 %copy-done = f32[3,3,3,128,128]{4,3,2,1,0:T(8,128)S(1)} copy-done((f32[3,3,3,128,128]{4,3,2,1,0:T(8,128)S(1)}, f32[3,3,3,128,128]{4,3,2,1,0:T(8,128)}, u32[]{:S(2)}) %copy-start) | copy-done | bytes 1769496
  2.1 0.0 copy-start.1
  2.1 1.5 %copy-done.1 = f32[3,3,3,128,128]{4,3,2,1,0:T(8,128)S(1)} copy-done((f32[3,3,3,128,128]{4,3,2,1,0:T(8,128)S(1)}, f32[3,3,3,128,128]{4,3,2,1,0:T(8,128)}, u32[]{:S(2)}) %copy-start.1) | copy-done | bytes 1769496
  3.6 0.0 copy-start.2
  3.6 0.9 %copy-done.2 = f32[4,2,32,128]{3,2,1,0:T(8,128)S(1)} copy-done((f32[4,2,32,128]{3,2,1,0:T(8,128)S(1)}, f32[4,2,32,128]{3,2,1,0:T(8,128)}, u32[]{:S(2)}) %copy-start.2) | copy-done | bytes 131096
  4.5 0.0 copy-start.3
  4.5 0.9 %copy-done.3 = f32[4,2,32,128]{3,2,1,0:T(8,128)S(1)} copy-done((f32[4,2,32,128]{3,2,1,0:T(8,128)S(1)}, f32[4,2,32,128]{3,2,1,0:T(8,128)}, u32[]{:S(2)}) %copy-start.3) | copy-done | bytes 131096
  5.4 74.1 %shard_map.75 = (f32[4,2,32,128]{3,2,1,0:T(8,128)S(1)}, f32[4,2,32,128]{3,2,1,0:T(8,128)S(1)}, f32[2,27,16,8,128]{4,3,2,1,0:T(8,128)S(1)}) custom-call(f32[4,2,32,128]{3,2,1,0:T(8,128)S(1)} %copy-done.2, f32[4,2,32,128]{3,2,1,0:T(8,128)S(1)} %copy-done.3, f32[27,128,128]{2,1,0:T(8,128)S(1)} %bitcast.4, f32[27,128,128]{2,1,0:T(8,128)S(1)} %bitcast.5), custom_call_target="tpu_custom_call" | custom-call | flops 5435817984 | bytes 8388608 | tf_op jit(solution)/shard_map/pallas_call | solution.py:309
  79.5 1.9 %shard_map.76 = (f32[4,2,32,128]{3,2,1,0:T(8,128)}, f32[4,2,32,128]{3,2,1,0:T(8,128)}, f32[27,16,8,128]{3,2,1,0:T(8,128)}, f32[27,16,8,128]{3,2,1,0:T(8,128)}) custom-call(f32[4,2,32,128]{3,2,1,0:T(8,128)S(1)} %get-tuple-element.11.block_ref, f32[4,2,32,128]{3,2,1,0:T(8,128)S(1)} %get-tuple-element.12.gclip_ref, ...), custom_call_target="tpu_custom_call" | custom-call | bytes 8388608 | tf_op jit(solution)/shard_map/pallas_call | solution.py:338
Async XLA Ops:
  0.6 1.5 %copy-start = (f32[3,3,3,128,128]{4,3,2,1,0:T(8,128)S(1)}, f32[3,3,3,128,128]{4,3,2,1,0:T(8,128)}, u32[]{:S(2)}) copy-start(f32[3,3,3,128,128]{4,3,2,1,0:T(8,128)} %param.5) | copy-start | bytes 5308420
  2.1 1.5 %copy-start.1 = (f32[3,3,3,128,128]{4,3,2,1,0:T(8,128)S(1)}, f32[3,3,3,128,128]{4,3,2,1,0:T(8,128)}, u32[]{:S(2)}) copy-start(f32[3,3,3,128,128]{4,3,2,1,0:T(8,128)} %param.6) | copy-start | bytes 5308420
  3.6 0.9 %copy-start.2 = (f32[4,2,32,128]{3,2,1,0:T(8,128)S(1)}, f32[4,2,32,128]{3,2,1,0:T(8,128)}, u32[]{:S(2)}) copy-start(f32[4,2,32,128]{3,2,1,0:T(8,128)} %clip_ref.1) | copy-start | bytes 393220
  4.5 0.9 %copy-start.3 = (f32[4,2,32,128]{3,2,1,0:T(8,128)S(1)}, f32[4,2,32,128]{3,2,1,0:T(8,128)}, u32[]{:S(2)}) copy-start(f32[4,2,32,128]{3,2,1,0:T(8,128)} %cot_ref.1) | copy-start | bytes 393220

commit v3 on v2

--- a/solution.py
+++ b/solution.py
@@ -10,10 +10,25 @@
 BF16 = jnp.bfloat16
 TAPS = [(a, b, c) for a in range(3) for b in range(3) for c in range(3)]
 GROUPS = [TAPS[0:8], TAPS[8:16], TAPS[16:24], TAPS[24:27]]
-STREAMS = [(0, 4, True), (4, 4, False), (8, 4, True), (12, 3, False), (15, 3, True), (18, 3, False), (21, 3, True), (24, 3, False)]
-PHASES = (0.0, 4.9, 8.4, 13.4, 18.4, 22.0, 27.0, 28.0)
-STEP = 1.9
-COPIES = 320
+STREAMS = []
+
+
+def plan():
+    first = 0
+    for k, (along_x, along_y) in enumerate(((3, 3), (3, 3), (3, 2), (2, 2))):
+        begin = (0.1, 0.3, 5.7, 7.7)[k]
+        arrive = 0.6 + 1.9 * (k + 1) + 3.0
+        late = [arrive + t for t in (0.0, 3.8, 8.8, 13.8, 17.6, 22.8, 23.8)]
+        for n, (axis, count) in enumerate((("x", along_x), ("y", along_y))):
+            STREAMS.append((first, count, axis, [0.05 * n + t for t in [0.2 * k, begin] + late]))
+            first += count
+    for k in range(2):
+        STREAMS.append((first, 3, "z", [0.35 + 0.25 * k + t for t in (0.0, 0.1, 8.0 + 3.0 * k, 13.0 + 3.0 * k, 18.0 + 3.0 * k, 26.0 + 3.0 * k, 27.0 + 3.0 * k)]))
+        first += 3
+
+
+plan()
+COPIES = 400
 Q = 1.0 / 256.0
 
 
@@ -29,7 +44,7 @@
 def kernel(
     clip_ref, cot_ref, k1_ref, k2_ref,
     block_ref, gclip_ref, sums,
-    kf, kh, kl, ext, ext2, cols, acc, pre, fixed, part, r1, r2, rz,
+    kf, kh, kl, ext, ext2, cols, acc, pre, fixed, part, r1, r2, rz, c1, c2,
     send_sem, recv_sem, load_sem,
 ):
     tm = lax.axis_index("tm")
@@ -54,8 +69,8 @@
     peers = [partner, (tm, outer_row)]
     for t in (tm_next, tm_prev):
         peers += [(t, rows), (t, partner_row), (t, outer_row)]
-    for d in range(1, 4):
-        peers += [at(x + d, y, z), at(x, y + d, z)]
+    plane = [(d % 4, d // 4) for d in range(1, 16)]
+    peers += [at(x + dx, y + dy, z) for dx, dy in plane]
     peers += [at(x, y, lax.rem(z + d, 8)) for d in range(1, 8)]
     barrier = pltpu.get_barrier_semaphore()
     for peer in peers:
@@ -218,6 +233,7 @@
 
         for tap in TAPS[first : first + count]:
             gradient(tap)
+        yield
         sent = [put(part.at[taps, pl.ds(4 * p_of[d], 4)], r1.at[d - 1, taps], ring[d - 1]) for d in (1, 2, 3)]
         yield
         for copy in sent:
@@ -256,6 +272,58 @@
         for d in (1, 2, 3):
             sent[d - 1].wait_recv()
             across.append(same(mine.at[taps, pl.ds(4 * p_of[4 - d], 4)], partner))
+        yield
+        for copy in across:
+            copy.wait_recv()
+
+    def stream_z(which, first, count):
+        taps = pl.ds(first, count)
+        got = pl.ds((which - 8) * count, count)
+        z_of = [lax.rem(z + d, 8) for d in range(8)]
+        mine = sums.at[core]
+
+        def owned(xx, yy):
+            o = lax.rem(lax.rem(xx, 4) + 4 * lax.rem(yy, 4) + 64 - 6 * (which - 8), 16)
+            return o < 2 * count, first + lax.rem(lax.div(o, 2), count), 2 * z + lax.rem(o, 2)
+
+        for tap in TAPS[first : first + count]:
+            gradient(tap)
+        yield
+        sent = [put(part.at[taps, pl.ds(2 * z_of[d], 2)], c1.at[d - 1, got], at(x, y, z_of[d])) for d in range(1, 8)]
+        yield
+        total = part[taps, pl.ds(2 * z, 2)]
+        for d in range(1, 8):
+            sent[d - 1].wait_recv()
+            total = total + c1[d - 1, got]
+        part[taps, pl.ds(2 * z, 2)] = total
+        sent = []
+        for n, (dx, dy) in enumerate(plane):
+            owns, tap, tile = owned(x + dx, y + dy)
+            sent.append(put(part.at[tap, tile], c2.at[which - 8, n], at(x + dx, y + dy, z), owns))
+        yield
+        owns, tap, tile = owned(x, y)
+
+        @pl.when(owns)
+        def _():
+            total = part[tap, tile]
+            for n in range(15):
+                sent[n].wait_recv()
+                total = total + c2[which - 8, n]
+            mine[tap, tile] = total * Q
+
+        done = mine.at[tap, tile]
+        sent = [put(done, done, at(x + dx, y + dy, z), owns) for dx, dy in plane]
+        yield
+        for n, (dx, dy) in enumerate(plane):
+            pl.when(owned(x + 4 - dx, y + 4 - dy)[0])(sent[n].wait_recv)
+        done = mine.at[taps, pl.ds(2 * z, 2)]
+        sent = [put(done, done, at(x, y, z_of[d])) for d in range(1, 8)]
+        across = [put(done, done, partner)]
+        yield
+        for d in range(1, 8):
+            sent[d - 1].wait_recv()
+            done = mine.at[taps, pl.ds(2 * z_of[8 - d], 2)]
+            across.append(put(done, done, partner))
         yield
         for copy in across:
             copy.wait_recv()
@@ -270,18 +338,17 @@
             out[...] = field[n, own_frames, own] + convolved()
             yield
 
-    running = [stream(n, *one) for n, one in enumerate(STREAMS)]
+    running, order = [], []
+    for n, (first, count, axis, times) in enumerate(STREAMS):
+        running.append(stream_z(n, first, count) if axis == "z" else stream(n, first, count, axis == "x"))
+        order += [(time, n) for time in times]
     finishing = finish()
-    order = []
-    for n in range(len(STREAMS)):
-        for phase, start in enumerate(PHASES):
-            order.append(((n // 2) * (STEP if phase else 0.6) + start, phase, n))
     halo2 = []
-    for when, phase, n in sorted(order):
-        if phase and not halo2:
+    for time, n in sorted(order):
+        if time > 5.9 and not halo2:
             halo2 += to_others(ext2)
         next(running[n], None)
-        if when > 6.0 and n % 2:
+        if time > 11.0:
             next(finishing, None)
     for _ in finishing:
         pass
@@ -294,7 +361,10 @@
 
 def copy_out(block_ref, gclip_ref, sums, block_out, gclip_out, one_out, two_out, sem):
     copies = []
-    for src, dst in ((sums.at[1], one_out), (sums.at[0], two_out), (block_ref, block_out), (gclip_ref, gclip_out)):
+    pieces = [(block_ref, block_out), (gclip_ref, gclip_out)]
+    for n, out in ((1, one_out), (0, two_out)):
+        pieces += [(sums.at[n, pl.ds(9 * i, 9)], out.at[pl.ds(9 * i, 9)]) for i in range(3)]
+    for src, dst in pieces:
         copies.append(pltpu.make_async_copy(src, dst, sem.at[len(copies)]))
         copies[-1].start()
     for copy in copies:
@@ -324,7 +394,9 @@
             pltpu.VMEM((27, 16, 8, 128), F32),
             pltpu.VMEM((3, 27, 4, 8, 128), F32),
             pltpu.VMEM((3, 27, 8, 128), F32),
-            pltpu.VMEM((len(STREAMS), 7, 8, 128), F32),
+            pltpu.VMEM((8, 7, 8, 128), F32),
+            pltpu.VMEM((7, 6, 2, 8, 128), F32),
+            pltpu.VMEM((2, 15, 8, 128), F32),
             pltpu.SemaphoreType.DMA((COPIES,)),
             pltpu.SemaphoreType.DMA((COPIES,)),
             pltpu.SemaphoreType.DMA((4,)),
@@ -333,14 +405,14 @@
             collective_id=0, has_side_effects=True, vmem_limit_bytes=32 * 1024 * 1024
         ),
         cost_estimate=pl.CostEstimate(flops=6 * 4 * 226492416, bytes_accessed=8 * 1024 * 1024, transcendentals=32768),
-    )(clip, cotangent, kernel_one.reshape(27, 128, 128), kernel_two.reshape(27, 128, 128))
+    )(*(pltpu.with_memory_space_constraint(a, pltpu.HBM) for a in (clip, cotangent, kernel_one.reshape(27, 128, 128), kernel_two.reshape(27, 128, 128))))
     grad = jax.ShapeDtypeStruct((27, 16, 8, 128), F32)
     block_out, grad_clip, grad_one, grad_two = pl.pallas_call(
         copy_out,
         out_shape=(field, field, grad, grad),
         in_specs=[anywhere] * 3,
         out_specs=(hbm,) * 4,
-        scratch_shapes=[pltpu.SemaphoreType.DMA((4,))],
+        scratch_shapes=[pltpu.SemaphoreType.DMA((8,))],
         compiler_params=pltpu.CompilerParams(vmem_limit_bytes=1024 * 1024),
         cost_estimate=pl.CostEstimate(flops=0, bytes_accessed=8 * 1024 * 1024, transcendentals=0),
     )(block_out, grad_clip, sums)

time: 81.6 us -> 76.7 us (0.940)
  local copies, waits for them, and re-layouts: 4.75 us -> 0 us
    unnamed x8 -> x0, local copies, waits for them, and re-layouts: 4.75 us -> none
where the time goes in v3:
time: 76.7 us; the launch traced here: 76.6 us
  Pallas kernels  75.8 us (99%)
  between operations  0.8 us (1%)
    pallas_call x1, Pallas kernels, per_device(): pl.pallas_call(kernel, out_shape=(field, field, jax.ShapeDtypeStruct((2,...  73.9 us
    pallas_call x1, Pallas kernels, per_device(): pl.pallas_call(copy_out, out_shape=(field, field, grad, grad), in_specs=[...  1.94 us

profile of v3, /device:TPU:1, one launch (start us, length us, event | category | flops | bytes accessed | tf_op | source)
XLA Modules:
  0.0 76.6 jit_solution(3214878156601423971)
XLA Ops:
  0.6 73.9 %shard_map.75 = (f32[4,2,32,128]{3,2,1,0:T(8,128)S(1)}, f32[4,2,32,128]{3,2,1,0:T(8,128)S(1)}, f32[2,27,16,8,128]{4,3,2,1,0:T(8,128)S(1)}) custom-call(f32[4,2,32,128]{3,2,1,0:T(8,128)} %clip_ref.1, f32[4,2,32,128]{3,2,1,0:T(8,128)} %cot_ref.1, f32[27,128,128]{2,1,0:T(8,128)} %bitcast.4, f32[27,128,128]{2,1,0:T(8,128)} %bitcast.5), custom_call_target="tpu_custom_call" | custom-call | flops 5435817984 | bytes 8388608 | tf_op jit(solution)/shard_map/pallas_call | solution.py:379
  74.5 1.9 %shard_map.76 = (f32[4,2,32,128]{3,2,1,0:T(8,128)}, f32[4,2,32,128]{3,2,1,0:T(8,128)}, f32[27,16,8,128]{3,2,1,0:T(8,128)}, f32[27,16,8,128]{3,2,1,0:T(8,128)}) custom-call(f32[4,2,32,128]{3,2,1,0:T(8,128)S(1)} %get-tuple-element.11.block_ref, f32[4,2,32,128]{3,2,1,0:T(8,128)S(1)} %get-tuple-element.12.gclip_ref, ...), custom_call_target="tpu_custom_call" | custom-call | bytes 8388608 | tf_op jit(solution)/shard_map/pallas_call | solution.py:410

commit v4 on v3

--- a/solution.py
+++ b/solution.py
@@ -44,7 +44,7 @@
 def kernel(
     clip_ref, cot_ref, k1_ref, k2_ref,
     block_ref, gclip_ref, sums,
-    kf, kh, kl, ext, ext2, cols, acc, pre, fixed, part, r1, r2, rz, c1, c2,
+    kf, kh, kl, ext, ext2, cols, acc, pre, d_active, fixed, part, r1, r2, rz, c1, c2,
     send_sem, recv_sem, load_sem,
 ):
     tm = lax.axis_index("tm")
@@ -101,16 +101,19 @@
         return [put(field.at[n, mine, own], field.at[n, mine, own], partner) for n, mine, _, _, _ in sides]
 
     def to_others(field):
-        out = []
-        for n, mine, src, dst, there in sides:
-            out.append(put(field.at[n, src, own], field.at[n, dst, own], (there, rows)))
-            out.append(put(field.at[n, mine, edge], field.at[n, mine, edge_there], (tm, outer_row)))
-            out.append(put(field.at[n, src, edge], field.at[n, dst, edge_there], (there, outer_row)))
-            out.append(put(field.at[n, src, inner], field.at[n, dst, inner], (there, partner_row)))
-        return out
-
-    halo = to_others(ext)
+        near, far = [], []
+        for n, mine, _, _, _ in sides:
+            near.append(put(field.at[n, mine, edge], field.at[n, mine, edge_there], (tm, outer_row)))
+        for n, _, src, dst, there in sides:
+            far.append([
+                put(field.at[n, src, edge], field.at[n, dst, edge_there], (there, outer_row)),
+                put(field.at[n, src, inner], field.at[n, dst, inner], (there, partner_row)),
+                put(field.at[n, src, own], field.at[n, dst, own], (there, rows)),
+            ])
+        return near, far
+
     beside = to_partner(ext)
+    near, far = to_others(ext)
 
     for load in loads[2:]:
         load.wait()
@@ -121,20 +124,11 @@
         return 0
 
     lax.fori_loop(0, 27, split_tap, 0)
-    for copy in halo + beside:
-        copy.wait_recv()
-    halo_frames, own_frames = pl.ds(4 * core, 2), pl.ds(2 - 2 * core, 4)
-    outer_rows = pl.ds(4 * core, 2)
-    passed = [
-        put(ext.at[core, halo_frames, outer_rows], ext.at[core, halo_frames, outer_rows], partner),
-        put(ext.at[core, own_frames, 5 * core], ext.at[core, own_frames, 5 * core], partner),
-    ]
-
     at_column = lax.broadcasted_iota(jnp.int32, (32, 128), 0)
 
-    def columns(field, n, row):
+    def columns(field, n, row, frames):
         inside = jnp.logical_not(((row == 0) & (y == 0)) | ((row == 5) & (y == 3)))
-        for f in range(6):
+        for f in frames:
             keep = inside
             if n == 0 and f < 2:
                 keep = keep & (tm > 0)
@@ -148,13 +142,14 @@
                 cols[n, h, 1, f, row] = piece.astype(BF16)
                 cols[n, h, 2, f, row] = jnp.where(at_column == 31, 0.0, pltpu.roll(piece, 31, 0)).astype(BF16)
 
-    def convolve(n, kernel_at, turned):
+    def convolve(n, kernel_at, turned, first):
         for g, group in enumerate(GROUPS):
             left, right = [], []
             for a, b, c in group:
                 at_tap = tap_index((a, b, c))
                 i, j, k = (2 - a, 2 - b, 2 - c) if turned else (a, b, c)
-                window = [cols[n, h, k, i : i + 4, pl.ds(2 * core + j, 2)].reshape(256, 128) for h in range(2)]
+                frames = slice(i + first, i + first + 2)
+                window = [cols[n, h, k, frames, pl.ds(2 * core + j, 2)].reshape(128, 128) for h in range(2)]
                 left.append(jnp.concatenate(window, 0))
                 right.append(jnp.concatenate([kh[kernel_at, at_tap], kl[kernel_at, at_tap]], 0 if turned else 1))
             left = jnp.concatenate(left, 1)
@@ -167,27 +162,45 @@
             yield
 
     def convolved():
-        total = acc[0:256, 0:128] + (acc[0:256, 128:256] + acc[256:512, 0:128]) + acc[256:512, 128:256]
-        return total.reshape(4, 2, 32, 128)
-
-    def near_columns(field, n):
+        total = acc[0:128, 0:128] + (acc[0:128, 128:256] + acc[128:256, 0:128]) + acc[128:256, 128:256]
+        return total.reshape(2, 2, 32, 128)
+
+    def near_columns(field, n, frames):
         def one(j, _):
-            columns(field, n, 2 * core + j)
+            columns(field, n, 2 * core + j, frames)
             return 0
 
         lax.fori_loop(0, 4, one, 0)
 
-    near_columns(ext, 0)
-    for _ in convolve(0, 0, False):
-        pass
-    pre[...] = convolved()
-    near_columns(ext, 1)
-    for _ in convolve(1, 1, True):
-        pass
+    own_of, other_of = (range(2, 6), range(0, 4)), (range(0, 2), range(4, 6))
+    early, late = (2, 0), (0, 2)
+
+    for copy in beside + near:
+        copy.wait_recv()
+    for n, into in ((0, pre), (1, d_active)):
+        near_columns(ext, n, own_of[n])
+        for _ in convolve(n, n, n == 1, early[n]):
+            pass
+        into[early[n] : early[n] + 2] = convolved()
+    for copies in far:
+        for copy in copies:
+            copy.wait_recv()
+    halo_frames, own_frames = pl.ds(4 * core, 2), pl.ds(2 - 2 * core, 4)
+    outer_rows = pl.ds(4 * core, 2)
+    passed = [
+        put(ext.at[core, halo_frames, outer_rows], ext.at[core, halo_frames, outer_rows], partner),
+        put(ext.at[core, own_frames, 5 * core], ext.at[core, own_frames, 5 * core], partner),
+    ]
+
+    for n, into in ((0, pre), (1, d_active)):
+        near_columns(ext, n, other_of[n])
+        for _ in convolve(n, n, n == 1, late[n]):
+            pass
+        into[late[n] : late[n] + 2] = convolved()
     v = pre[...]
     s = jax.nn.sigmoid(v)
     ext2[0, 2:6, own] = v * s
-    ext2[1, 0:4, own] = convolved() * s * (1.0 + v * (1.0 - s))
+    ext2[1, 0:4, own] = d_active[...] * s * (1.0 + v * (1.0 - s))
     swap = to_partner(ext2)
 
     for copy in passed:
@@ -196,12 +209,12 @@
     @pl.when(core == 0)
     def _():
         for row in (4, 5):
-            columns(ext, 1, row)
+            columns(ext, 1, row, range(6))
 
     @pl.when(core == 1)
     def _():
         for row in (0, 1):
-            columns(ext, 0, row)
+            columns(ext, 0, row, range(6))
 
     for copy in swap:
         copy.wait_recv()
@@ -329,14 +342,21 @@
             copy.wait_recv()
 
     def finish():
-        for n, field, out, kernel_at, own_frames in ((0, ext, block_ref, 1, pl.ds(2, 4)), (1, ext, gclip_ref, 0, pl.ds(0, 4))):
-            for copy in halo2[4 * n : 4 * n + 4]:
-                copy.wait_recv()
-            near_columns(ext2, n)
+        for n, out in ((0, block_ref), (1, gclip_ref)):
+            near2, far2 = halo2
+            near2[n].wait_recv()
+            near_columns(ext2, n, own_of[n])
             yield
-            yield from convolve(n, kernel_at, n == 1)
-            out[...] = field[n, own_frames, own] + convolved()
-            yield
+            for half in (early[n], late[n]):
+                yield from convolve(n, 1 - n, n == 1, half)
+                shown = half + 2 * (1 - n)
+                out[half : half + 2] = ext[n, shown : shown + 2, own] + convolved()
+                yield
+                if half == early[n]:
+                    for copy in far2[n]:
+                        copy.wait_recv()
+                    near_columns(ext2, n, other_of[n])
+                    yield
 
     running, order = [], []
     for n, (first, count, axis, times) in enumerate(STREAMS):
@@ -344,12 +364,14 @@
         order += [(time, n) for time in times]
     finishing = finish()
     halo2 = []
-    for time, n in sorted(order):
-        if time > 5.9 and not halo2:
+    order.sort()
+    for at_event, (time, n) in enumerate(order):
+        if time > 9.0 and not halo2:
             halo2 += to_others(ext2)
         next(running[n], None)
-        if time > 11.0:
-            next(finishing, None)
+        if time > 14.0 and at_event + 1 < len(order):
+            for _ in range(int((order[at_event + 1][0] - time) / 0.25)):
+                next(finishing, None)
     for _ in finishing:
         pass
     for copy, sends in started:
@@ -388,7 +410,8 @@
             pltpu.VMEM((2, 6, 6, 32, 128), F32),
             pltpu.VMEM((2, 6, 6, 32, 128), F32),
             pltpu.VMEM((2, 2, 3, 6, 6, 32, 128), BF16),
-            pltpu.VMEM((512, 256), F32),
+            pltpu.VMEM((256, 256), F32),
+            pltpu.VMEM((4, 2, 32, 128), F32),
             pltpu.VMEM((4, 2, 32, 128), F32),
             pltpu.VMEM((256, 512), BF16),
             pltpu.VMEM((27, 16, 8, 128), F32),

time: 76.7 us -> 71.7 us (0.935)
  Pallas kernels: 75.8 us -> 70.8 us
    pallas_call x1, Pallas kernels: 73.9 us -> 68.9 us  [per_device(): pl.pallas_call(kernel, out_shape=(field, field, jax.ShapeDtypeStruct((2,...]
where the time goes in v4:
time: 71.7 us; the launch traced here: 71.6 us
  Pallas kernels  70.8 us (99%)
  between operations  0.8 us (1%)
    pallas_call x1, Pallas kernels, per_device(): pl.pallas_call(kernel, out_shape=(field, field, jax.ShapeDtypeStruct((2,...  68.9 us
    pallas_call x1, Pallas kernels, per_device(): pl.pallas_call(copy_out, out_shape=(field, field, grad, grad), in_specs=[...  1.94 us

profile of v4, /device:TPU:1, one launch (start us, length us, event | category | flops | bytes accessed | tf_op | source)
XLA Modules:
  0.0 71.6 jit_solution(6361580958708723557)
XLA Ops:
  0.6 68.9 %shard_map.75 = (f32[4,2,32,128]{3,2,1,0:T(8,128)S(1)}, f32[4,2,32,128]{3,2,1,0:T(8,128)S(1)}, f32[2,27,16,8,128]{4,3,2,1,0:T(8,128)S(1)}) custom-call(f32[4,2,32,128]{3,2,1,0:T(8,128)} %clip_ref.1, f32[4,2,32,128]{3,2,1,0:T(8,128)} %cot_ref.1, f32[27,128,128]{2,1,0:T(8,128)} %bitcast.4, f32[27,128,128]{2,1,0:T(8,128)} %bitcast.5), custom_call_target="tpu_custom_call" | custom-call | flops 5435817984 | bytes 8388608 | tf_op jit(solution)/shard_map/pallas_call | solution.py:401
  69.5 1.9 %shard_map.76 = (f32[4,2,32,128]{3,2,1,0:T(8,128)}, f32[4,2,32,128]{3,2,1,0:T(8,128)}, f32[27,16,8,128]{3,2,1,0:T(8,128)}, f32[27,16,8,128]{3,2,1,0:T(8,128)}) custom-call(f32[4,2,32,128]{3,2,1,0:T(8,128)S(1)} %get-tuple-element.11.block_ref, f32[4,2,32,128]{3,2,1,0:T(8,128)S(1)} %get-tuple-element.12.gclip_ref, ...), custom_call_target="tpu_custom_call" | custom-call | bytes 8388608 | tf_op jit(solution)/shard_map/pallas_call | solution.py:433

commit v5 on v4

--- a/solution.py
+++ b/solution.py
@@ -11,24 +11,29 @@
 TAPS = [(a, b, c) for a in range(3) for b in range(3) for c in range(3)]
 GROUPS = [TAPS[0:8], TAPS[8:16], TAPS[16:24], TAPS[24:27]]
 STREAMS = []
+PAIRS = ((3, 3), (3, 3), (3, 3), (2, 2))
+BEGIN = (0.1, 0.3, 0.5, 5.7)
+ALONG_Z = (5,)
 
 
 def plan():
-    first = 0
-    for k, (along_x, along_y) in enumerate(((3, 3), (3, 3), (3, 2), (2, 2))):
-        begin = (0.1, 0.3, 5.7, 7.7)[k]
-        arrive = 0.6 + 1.9 * (k + 1) + 3.0
-        late = [arrive + t for t in (0.0, 3.8, 8.8, 13.8, 17.6, 22.8, 23.8)]
-        for n, (axis, count) in enumerate((("x", along_x), ("y", along_y))):
-            STREAMS.append((first, count, axis, [0.05 * n + t for t in [0.2 * k, begin] + late]))
+    first, sent = 0, 0
+    for k, counts in enumerate(PAIRS):
+        sent += counts[0]
+        arrive = 3.6 + 0.6 * sent
+        late = [arrive + t for t in (0.0, 3.8, 8.8, 13.8, 17.6, 20.8 + 0.6 * counts[0], 99.0)]
+        for n, count in enumerate(counts):
+            STREAMS.append((k * 2 + n, first, count, "xy"[n], [0.05 * n + t for t in [0.2 * k, BEGIN[k]] + late]))
             first += count
-    for k in range(2):
-        STREAMS.append((first, 3, "z", [0.35 + 0.25 * k + t for t in (0.0, 0.1, 8.0 + 3.0 * k, 13.0 + 3.0 * k, 18.0 + 3.0 * k, 26.0 + 3.0 * k, 27.0 + 3.0 * k)]))
-        first += 3
+    sent = 0
+    for k, count in enumerate(ALONG_Z):
+        begin, sent = 0.35 + 0.25 * k, sent + count
+        STREAMS.append((k, first, count, "z", [begin + t for t in (0.0, 0.1, 4.6 + 1.1 * sent, 9.6 + 1.1 * sent, 14.6 + 1.1 * sent, 19.2 + 2.2 * sent, 99.5)]))
+        first += count
 
 
 plan()
-COPIES = 400
+SEMAPHORES = (22, 64)
 Q = 1.0 / 256.0
 
 
@@ -79,37 +84,58 @@
         load.wait()
     pl.semaphore_wait(barrier, len(peers))
 
-    started = []
-
-    def put(src, dst, device, sends=None):
-        n = len(started)
-        copy = pltpu.make_async_remote_copy(
-            src_ref=src, dst_ref=dst, send_sem=send_sem.at[n], recv_sem=recv_sem.at[n],
+    taken = [0, 0]
+
+    def new(side):
+        taken[side] += 1
+        return taken[side] - 1
+
+    def group():
+        return new(0), new(1)
+
+    def copy_of(src, dst, device, sems):
+        return pltpu.make_async_remote_copy(
+            src_ref=src, dst_ref=dst, send_sem=send_sem.at[sems[0]], recv_sem=recv_sem.at[sems[1]],
             device_id=device, device_id_type=MESH,
         )
+
+    def put(src, dst, device, sems, sends=None):
+        copy = copy_of(src, dst, device, sems)
         if sends is None:
             copy.start()
         else:
             pl.when(sends)(copy.start)
-        started.append((copy, sends))
-        return copy
+
+    def arrived(ref, sems):
+        copy_of(ref, ref, partner, sems).wait_recv()
+
+    def left(ref, sems):
+        copy_of(ref, ref, partner, sems).wait_send()
+
+    to_leave = []
 
     edge, edge_there, inner = 1 + 3 * core, 5 - 5 * core, 2 + core
     sides = ((0, pl.ds(2, 4), pl.ds(4, 2), pl.ds(0, 2), tm_next), (1, pl.ds(0, 4), pl.ds(0, 2), pl.ds(4, 2), tm_prev))
 
     def to_partner(field):
-        return [put(field.at[n, mine, own], field.at[n, mine, own], partner) for n, mine, _, _, _ in sides]
+        sems = group()
+        for n, mine, _, _, _ in sides:
+            put(field.at[n, mine, own], field.at[n, mine, own], partner, sems)
+        to_leave.append((field.at[:, 0:4, 0:2], sems))
+        return to_leave[-1]
 
     def to_others(field):
         near, far = [], []
         for n, mine, _, _, _ in sides:
-            near.append(put(field.at[n, mine, edge], field.at[n, mine, edge_there], (tm, outer_row)))
+            near.append((field.at[n, 0:4, 0], group()))
+            put(field.at[n, mine, edge], field.at[n, mine, edge_there], (tm, outer_row), near[n][1])
         for n, _, src, dst, there in sides:
-            far.append([
-                put(field.at[n, src, edge], field.at[n, dst, edge_there], (there, outer_row)),
-                put(field.at[n, src, inner], field.at[n, dst, inner], (there, partner_row)),
-                put(field.at[n, src, own], field.at[n, dst, own], (there, rows)),
-            ])
+            sems = group()
+            put(field.at[n, src, edge], field.at[n, dst, edge_there], (there, outer_row), sems)
+            put(field.at[n, src, inner], field.at[n, dst, inner], (there, partner_row), sems)
+            put(field.at[n, src, own], field.at[n, dst, own], (there, rows), sems)
+            far.append((field.at[n, 0:2, 0:4], sems))
+        to_leave.extend(near + far)
         return near, far
 
     beside = to_partner(ext)
@@ -175,22 +201,21 @@
     own_of, other_of = (range(2, 6), range(0, 4)), (range(0, 2), range(4, 6))
     early, late = (2, 0), (0, 2)
 
-    for copy in beside + near:
-        copy.wait_recv()
+    for copies in [beside] + near:
+        arrived(*copies)
     for n, into in ((0, pre), (1, d_active)):
         near_columns(ext, n, own_of[n])
         for _ in convolve(n, n, n == 1, early[n]):
             pass
         into[early[n] : early[n] + 2] = convolved()
     for copies in far:
-        for copy in copies:
-            copy.wait_recv()
+        arrived(*copies)
     halo_frames, own_frames = pl.ds(4 * core, 2), pl.ds(2 - 2 * core, 4)
     outer_rows = pl.ds(4 * core, 2)
-    passed = [
-        put(ext.at[core, halo_frames, outer_rows], ext.at[core, halo_frames, outer_rows], partner),
-        put(ext.at[core, own_frames, 5 * core], ext.at[core, own_frames, 5 * core], partner),
-    ]
+    passed = (ext.at[0, 0:4, 0:2], group())
+    for mine in (ext.at[core, halo_frames, outer_rows], ext.at[core, own_frames, 5 * core]):
+        put(mine, mine, partner, passed[1])
+    to_leave.append(passed)
 
     for n, into in ((0, pre), (1, d_active)):
         near_columns(ext, n, other_of[n])
@@ -203,8 +228,7 @@
     ext2[1, 0:4, own] = d_active[...] * s * (1.0 + v * (1.0 - s))
     swap = to_partner(ext2)
 
-    for copy in passed:
-        copy.wait_recv()
+    arrived(*passed)
 
     @pl.when(core == 0)
     def _():
@@ -216,8 +240,7 @@
         for row in (0, 1):
             columns(ext, 0, row, range(6))
 
-    for copy in swap:
-        copy.wait_recv()
+    arrived(*swap)
     whole = ext2[core, own_frames, 1:5].reshape(512, 128)
     fixed[0:128], fixed[128:256] = split(whole.T)
 
@@ -227,6 +250,12 @@
         m = jnp.dot(fixed[...], jnp.concatenate(right, 1), preferred_element_type=F32)
         m = m[0:128, 0:128] + (m[0:128, 128:256] + m[128:256, 0:128]) + m[128:256, 128:256]
         part[tap_index(tap)] = jnp.where(core == 1, m.T, m).reshape(16, 8, 128)
+
+    ring_sends, ring2_sends, z_sends, back_z, back_ring2, back_ring, across_sends = (new(0) for _ in range(7))
+    across = (across_sends, new(1))
+
+    def same(ref, to, sems):
+        put(ref, ref, to, sems)
 
     def stream(which, first, count, x_first):
         taps = pl.ds(first, count)
@@ -241,110 +270,145 @@
         tap_at = [first + lax.rem(k, count) for k in place]
         z_of = [lax.rem(z + d, 8) for d in range(8)]
 
-        def same(ref, to):
-            return put(ref, ref, to)
-
         for tap in TAPS[first : first + count]:
             gradient(tap)
         yield
-        sent = [put(part.at[taps, pl.ds(4 * p_of[d], 4)], r1.at[d - 1, taps], ring[d - 1]) for d in (1, 2, 3)]
-        yield
-        for copy in sent:
-            copy.wait_recv()
+        sems = (ring_sends, new(1))
+        for d in (1, 2, 3):
+            put(part.at[taps, pl.ds(4 * p_of[d], 4)], r1.at[d - 1, taps], ring[d - 1], sems)
+        yield
+        arrived(r1.at[:, taps], sems)
         part[taps, pl.ds(4 * p, 4)] += r1[0, taps] + r1[1, taps] + r1[2, taps]
-        sent = [put(part.at[taps, 4 * p + s_of[d]], r2.at[d - 1, taps], ring2[d - 1]) for d in (1, 2, 3)]
-        yield
-        for copy in sent:
-            copy.wait_recv()
+        sems = (ring2_sends, new(1))
+        for d in (1, 2, 3):
+            put(part.at[taps, 4 * p + s_of[d]], r2.at[d - 1, taps], ring2[d - 1], sems)
+        yield
+        arrived(r2.at[:, taps], sems)
         part[taps, tile] += r2[0, taps] + r2[1, taps] + r2[2, taps]
-        sent = []
+        sems = (z_sends, new(1))
         for d in range(1, 8):
-            sent.append(put(part.at[tap_at[d], tile], rz.at[which, d - 1], at(x, y, z_of[d]), owns[d]))
+            put(part.at[tap_at[d], tile], rz.at[which, d - 1], at(x, y, z_of[d]), sems, owns[d])
         yield
 
         @pl.when(owns[0])
         def _():
+            arrived(rz.at[which], sems)
             total = part[tap_at[0], tile]
             for d in range(1, 8):
-                sent[d - 1].wait_recv()
                 total = total + rz[which, d - 1]
             mine[tap_at[0], tile] = total * Q
 
         done = mine.at[tap_at[0], tile]
-        sent = [put(done, done, at(x, y, z_of[d]), owns[0]) for d in range(1, 8)]
-        yield
+        sems = (back_z, new(1))
         for d in range(1, 8):
-            pl.when(owns[8 - d])(sent[d - 1].wait_recv)
-        sent = [same(mine.at[taps, tile], to) for to in ring2]
-        yield
-        for copy in sent:
-            copy.wait_recv()
-        sent = [same(mine.at[taps, pl.ds(4 * p, 4)], to) for to in ring]
-        across = [same(mine.at[taps, pl.ds(4 * p, 4)], partner)]
-        yield
-        for d in (1, 2, 3):
-            sent[d - 1].wait_recv()
-            across.append(same(mine.at[taps, pl.ds(4 * p_of[4 - d], 4)], partner))
-        yield
-        for copy in across:
-            copy.wait_recv()
+            put(done, done, at(x, y, z_of[d]), sems, owns[0])
+        yield
+
+        @pl.when(owns[0])
+        def _():
+            arrived(mine.at[pl.ds(first, count - 1), tile], sems)
+
+        @pl.when(jnp.logical_not(owns[0]))
+        def _():
+            arrived(mine.at[taps, tile], sems)
+
+        sems = (back_ring2, new(1))
+        for to in ring2:
+            same(mine.at[taps, tile], to, sems)
+        yield
+        arrived(r2.at[:, taps], sems)
+        sems = (back_ring, new(1))
+        chunks = [mine.at[taps, pl.ds(4 * i, 4)] for i in p_of]
+        for to in ring:
+            same(chunks[0], to, sems)
+        same(chunks[0], partner, across)
+        yield
+        arrived(r1.at[:, taps], sems)
+        for chunk in chunks[1:]:
+            same(chunk, partner, across)
+        yield
+
+    def streams_left():
+        count = sum(sum(pair) for pair in PAIRS)
+        each, more = divmod(count, 8)
+        left(r1.at[:, 0:count], (ring_sends, 0))
+        left(r1.at[:, 0:count], (back_ring, 0))
+        left(r2.at[:, 0:count], (ring2_sends, 0))
+        left(r2.at[:, 0:count], (back_ring2, 0))
+        for some, held in ((z < more, each + 1), (z >= more, each)):
+
+            @pl.when(some)
+            def _():
+                left(part.at[0 : count - held, 0], (z_sends, 0))
+                left(part.at[0 : 7 * held, 0], (back_z, 0))
 
     def stream_z(which, first, count):
         taps = pl.ds(first, count)
-        got = pl.ds((which - 8) * count, count)
+        got = pl.ds(first - 27 + sum(ALONG_Z), count)
         z_of = [lax.rem(z + d, 8) for d in range(8)]
         mine = sums.at[core]
 
         def owned(xx, yy):
-            o = lax.rem(lax.rem(xx, 4) + 4 * lax.rem(yy, 4) + 64 - 6 * (which - 8), 16)
+            o = lax.rem(lax.rem(xx, 4) + 4 * lax.rem(yy, 4) + 64 - 6 * which, 16)
             return o < 2 * count, first + lax.rem(lax.div(o, 2), count), 2 * z + lax.rem(o, 2)
+
+        def when_owned(one, other):
+            pl.when(owns)(one)
+            pl.when(jnp.logical_not(owns))(other)
 
         for tap in TAPS[first : first + count]:
             gradient(tap)
         yield
-        sent = [put(part.at[taps, pl.ds(2 * z_of[d], 2)], c1.at[d - 1, got], at(x, y, z_of[d])) for d in range(1, 8)]
-        yield
+        sems = group()
+        to_leave.append((c1.at[:, got], sems))
+        for d in range(1, 8):
+            put(part.at[taps, pl.ds(2 * z_of[d], 2)], c1.at[d - 1, got], at(x, y, z_of[d]), sems)
+        yield
+        arrived(c1.at[:, got], sems)
         total = part[taps, pl.ds(2 * z, 2)]
         for d in range(1, 8):
-            sent[d - 1].wait_recv()
             total = total + c1[d - 1, got]
         part[taps, pl.ds(2 * z, 2)] = total
-        sent = []
+        first_sems = group()
         for n, (dx, dy) in enumerate(plane):
             owns, tap, tile = owned(x + dx, y + dy)
-            sent.append(put(part.at[tap, tile], c2.at[which - 8, n], at(x + dx, y + dy, z), owns))
+            put(part.at[tap, tile], c2.at[which, n], at(x + dx, y + dy, z), first_sems, owns)
         yield
         owns, tap, tile = owned(x, y)
 
         @pl.when(owns)
         def _():
+            arrived(c2.at[which], first_sems)
             total = part[tap, tile]
             for n in range(15):
-                sent[n].wait_recv()
-                total = total + c2[which - 8, n]
+                total = total + c2[which, n]
             mine[tap, tile] = total * Q
 
         done = mine.at[tap, tile]
-        sent = [put(done, done, at(x + dx, y + dy, z), owns) for dx, dy in plane]
-        yield
-        for n, (dx, dy) in enumerate(plane):
-            pl.when(owned(x + 4 - dx, y + 4 - dy)[0])(sent[n].wait_recv)
+        second_sems = group()
+        for dx, dy in plane:
+            put(done, done, at(x + dx, y + dy, z), second_sems, owns)
+        yield
+        fewer, all_tiles = (part.at[0 : 2 * count - n, 0] for n in (1, 0))
+        when_owned(lambda: arrived(fewer, second_sems), lambda: arrived(all_tiles, second_sems))
         done = mine.at[taps, pl.ds(2 * z, 2)]
-        sent = [put(done, done, at(x, y, z_of[d])) for d in range(1, 8)]
-        across = [put(done, done, partner)]
-        yield
+        sems = group()
+        to_leave.append((c1.at[:, got], sems))
         for d in range(1, 8):
-            sent[d - 1].wait_recv()
-            done = mine.at[taps, pl.ds(2 * z_of[8 - d], 2)]
-            across.append(put(done, done, partner))
-        yield
-        for copy in across:
-            copy.wait_recv()
+            same(done, at(x, y, z_of[d]), sems)
+        same(done, partner, across)
+        yield
+        arrived(c1.at[:, got], sems)
+        for d in range(1, 8):
+            same(mine.at[taps, pl.ds(2 * z_of[d], 2)], partner, across)
+        yield
+        when_owned(lambda: left(fewer, first_sems), lambda: left(all_tiles, first_sems))
+        pl.when(owns)(lambda: left(c2.at[which], second_sems))
 
     def finish():
         for n, out in ((0, block_ref), (1, gclip_ref)):
             near2, far2 = halo2
-            near2[n].wait_recv()
+            arrived(*near2[n])
             near_columns(ext2, n, own_of[n])
             yield
             for half in (early[n], late[n]):
@@ -353,14 +417,13 @@
                 out[half : half + 2] = ext[n, shown : shown + 2, own] + convolved()
                 yield
                 if half == early[n]:
-                    for copy in far2[n]:
-                        copy.wait_recv()
+                    arrived(*far2[n])
                     near_columns(ext2, n, other_of[n])
                     yield
 
     running, order = [], []
-    for n, (first, count, axis, times) in enumerate(STREAMS):
-        running.append(stream_z(n, first, count) if axis == "z" else stream(n, first, count, axis == "x"))
+    for n, (which, first, count, axis, times) in enumerate(STREAMS):
+        running.append(stream_z(which, first, count) if axis == "z" else stream(which, first, count, axis == "x"))
         order += [(time, n) for time in times]
     finishing = finish()
     halo2 = []
@@ -374,11 +437,11 @@
                 next(finishing, None)
     for _ in finishing:
         pass
-    for copy, sends in started:
-        if sends is None:
-            copy.wait_send()
-        else:
-            pl.when(sends)(copy.wait_send)
+    arrived(sums.at[1 - core], across)
+    left(sums.at[core], across)
+    streams_left()
+    for ref, sems in to_leave:
+        left(ref, sems)
 
 
 def copy_out(block_ref, gclip_ref, sums, block_out, gclip_out, one_out, two_out, sem):
@@ -417,11 +480,11 @@
             pltpu.VMEM((27, 16, 8, 128), F32),
             pltpu.VMEM((3, 27, 4, 8, 128), F32),
             pltpu.VMEM((3, 27, 8, 128), F32),
-            pltpu.VMEM((8, 7, 8, 128), F32),
-            pltpu.VMEM((7, 6, 2, 8, 128), F32),
-            pltpu.VMEM((2, 15, 8, 128), F32),
-            pltpu.SemaphoreType.DMA((COPIES,)),
-            pltpu.SemaphoreType.DMA((COPIES,)),
+            pltpu.VMEM((2 * len(PAIRS), 7, 8, 128), F32),
+            pltpu.VMEM((7, sum(ALONG_Z) + 1, 2, 8, 128), F32),
+            pltpu.VMEM((len(ALONG_Z) + 1, 15, 8, 128), F32),
+            pltpu.SemaphoreType.DMA((SEMAPHORES[0],)),
+            pltpu.SemaphoreType.DMA((SEMAPHORES[1],)),
             pltpu.SemaphoreType.DMA((4,)),
         ],
         compiler_params=pltpu.CompilerParams(

time: 71.7 us -> 61.8 us (0.86)
  Pallas kernels: 70.8 us -> 61.1 us
    pallas_call x1, Pallas kernels: 68.9 us -> 59.1 us  [per_device(): pl.pallas_call(kernel, out_shape=(field, field, jax.ShapeDtypeStruct((2,...]
where the time goes in v5:
time: 61.8 us; the launch traced here: 61.7 us
  Pallas kernels  61.1 us (99%)
  between operations  0.64 us (1%)
    pallas_call x1, Pallas kernels, per_device(): pl.pallas_call(kernel, out_shape=(field, field, jax.ShapeDtypeStruct((2,...  59.1 us
    pallas_call x1, Pallas kernels, per_device(): pl.pallas_call(copy_out, out_shape=(field, field, grad, grad), in_specs=[...  1.94 us

profile of v5, /device:TPU:1, one launch (start us, length us, event | category | flops | bytes accessed | tf_op | source)
XLA Modules:
  0.0 61.7 jit_solution(18263768061880322378)
XLA Ops:
  0.6 59.1 %shard_map.75 = (f32[4,2,32,128]{3,2,1,0:T(8,128)S(1)}, f32[4,2,32,128]{3,2,1,0:T(8,128)S(1)}, f32[2,27,16,8,128]{4,3,2,1,0:T(8,128)S(1)}) custom-call(f32[4,2,32,128]{3,2,1,0:T(8,128)} %clip_ref.1, f32[4,2,32,128]{3,2,1,0:T(8,128)} %cot_ref.1, f32[27,128,128]{2,1,0:T(8,128)} %bitcast.4, f32[27,128,128]{2,1,0:T(8,128)} %bitcast.5), custom_call_target="tpu_custom_call" | custom-call | flops 5435817984 | bytes 8388608 | tf_op jit(solution)/shard_map/pallas_call | solution.py:464
  59.8 1.9 %shard_map.76 = (f32[4,2,32,128]{3,2,1,0:T(8,128)}, f32[4,2,32,128]{3,2,1,0:T(8,128)}, f32[27,16,8,128]{3,2,1,0:T(8,128)}, f32[27,16,8,128]{3,2,1,0:T(8,128)}) custom-call(f32[4,2,32,128]{3,2,1,0:T(8,128)S(1)} %get-tuple-element.11.block_ref, f32[4,2,32,128]{3,2,1,0:T(8,128)S(1)} %get-tuple-element.12.gclip_ref, ...), custom_call_target="tpu_custom_call" | custom-call | bytes 8388608 | tf_op jit(solution)/shard_map/pallas_call | solution.py:496

commit v6 on v5

--- a/solution.py
+++ b/solution.py
@@ -33,7 +33,7 @@
 
 
 plan()
-SEMAPHORES = (22, 64)
+SEMAPHORES = (23, 65)
 Q = 1.0 / 256.0
 
 
@@ -80,8 +80,6 @@
     barrier = pltpu.get_barrier_semaphore()
     for peer in peers:
         pl.semaphore_signal(barrier, inc=1, device_id=peer, device_id_type=MESH)
-    for load in loads[:2]:
-        load.wait()
     pl.semaphore_wait(barrier, len(peers))
 
     taken = [0, 0]
@@ -117,30 +115,35 @@
     edge, edge_there, inner = 1 + 3 * core, 5 - 5 * core, 2 + core
     sides = ((0, pl.ds(2, 4), pl.ds(4, 2), pl.ds(0, 2), tm_next), (1, pl.ds(0, 4), pl.ds(0, 2), pl.ds(4, 2), tm_prev))
 
-    def to_partner(field):
-        sems = group()
-        for n, mine, _, _, _ in sides:
-            put(field.at[n, mine, own], field.at[n, mine, own], partner, sems)
-        to_leave.append((field.at[:, 0:4, 0:2], sems))
-        return to_leave[-1]
-
-    def to_others(field):
+    def to_others(field, seen):
         near, far = [], []
         for n, mine, _, _, _ in sides:
             near.append((field.at[n, 0:4, 0], group()))
-            put(field.at[n, mine, edge], field.at[n, mine, edge_there], (tm, outer_row), near[n][1])
+            put(seen(n, mine, edge), field.at[n, mine, edge_there], (tm, outer_row), near[n][1])
         for n, _, src, dst, there in sides:
             sems = group()
-            put(field.at[n, src, edge], field.at[n, dst, edge_there], (there, outer_row), sems)
-            put(field.at[n, src, inner], field.at[n, dst, inner], (there, partner_row), sems)
-            put(field.at[n, src, own], field.at[n, dst, own], (there, rows), sems)
+            put(seen(n, src, edge), field.at[n, dst, edge_there], (there, outer_row), sems)
+            put(seen(n, src, inner), field.at[n, dst, inner], (there, partner_row), sems)
+            put(seen(n, src, own), field.at[n, dst, own], (there, rows), sems)
             far.append((field.at[n, 0:2, 0:4], sems))
         to_leave.extend(near + far)
         return near, far
 
-    beside = to_partner(ext)
-    near, far = to_others(ext)
-
+    def operand(n, frames, at_rows):
+        ref = (clip_ref, cot_ref)[n]
+        frames = pl.ds(frames.start - 2 * (1 - n), frames.size)
+        if at_rows is own:
+            return ref.at[frames]
+        return ref.at[frames, core if at_rows is edge else 1 - core]
+
+    near, far = to_others(ext, operand)
+    beside = (ext.at[:, 0:4, 0:2], group())
+    for n, mine, _, _, _ in sides:
+        put(operand(n, mine, own), ext.at[n, mine, own], partner, beside[1])
+    to_leave.append(beside)
+
+    for load in loads[:2]:
+        load.wait()
     for load in loads[2:]:
         load.wait()
 
@@ -168,27 +171,28 @@
                 cols[n, h, 1, f, row] = piece.astype(BF16)
                 cols[n, h, 2, f, row] = jnp.where(at_column == 31, 0.0, pltpu.roll(piece, 31, 0)).astype(BF16)
 
-    def convolve(n, kernel_at, turned, first):
-        for g, group in enumerate(GROUPS):
-            left, right = [], []
-            for a, b, c in group:
+    def convolve(n, kernel_at, turned, first, slot=0, groups=GROUPS, more=False):
+        for group_taps in groups:
+            lhs, rhs = [], []
+            for a, b, c in group_taps:
                 at_tap = tap_index((a, b, c))
                 i, j, k = (2 - a, 2 - b, 2 - c) if turned else (a, b, c)
                 frames = slice(i + first, i + first + 2)
                 window = [cols[n, h, k, frames, pl.ds(2 * core + j, 2)].reshape(128, 128) for h in range(2)]
-                left.append(jnp.concatenate(window, 0))
-                right.append(jnp.concatenate([kh[kernel_at, at_tap], kl[kernel_at, at_tap]], 0 if turned else 1))
-            left = jnp.concatenate(left, 1)
-            right = jnp.concatenate(right, 1 if turned else 0)
-            product = lax.dot_general(left, right, (((1,), (1 if turned else 0,)), ((), ())), preferred_element_type=F32)
-            if g == 0:
-                acc[...] = product
+                lhs.append(jnp.concatenate(window, 0))
+                rhs.append(jnp.concatenate([kh[kernel_at, at_tap], kl[kernel_at, at_tap]], 0 if turned else 1))
+            lhs = jnp.concatenate(lhs, 1)
+            rhs = jnp.concatenate(rhs, 1 if turned else 0)
+            product = lax.dot_general(lhs, rhs, (((1,), (1 if turned else 0,)), ((), ())), preferred_element_type=F32)
+            if more:
+                acc[slot] += product
             else:
-                acc[...] += product
+                acc[slot] = product
+            more = True
             yield
 
-    def convolved():
-        total = acc[0:128, 0:128] + (acc[0:128, 128:256] + acc[128:256, 0:128]) + acc[128:256, 128:256]
+    def convolved(slot=0):
+        total = acc[slot, 0:128, 0:128] + (acc[slot, 0:128, 128:256] + acc[slot, 128:256, 0:128]) + acc[slot, 128:256, 128:256]
         return total.reshape(2, 2, 32, 128)
 
     def near_columns(field, n, frames):
@@ -208,6 +212,9 @@
         for _ in convolve(n, n, n == 1, early[n]):
             pass
         into[early[n] : early[n] + 2] = convolved()
+    for n in range(2):
+        for _ in convolve(n, n, n == 1, late[n], 1 + n, [TAPS[18:26], TAPS[26:27]]):
+            pass
     for copies in far:
         arrived(*copies)
     halo_frames, own_frames = pl.ds(4 * core, 2), pl.ds(2 - 2 * core, 4)
@@ -219,14 +226,17 @@
 
     for n, into in ((0, pre), (1, d_active)):
         near_columns(ext, n, other_of[n])
-        for _ in convolve(n, n, n == 1, late[n]):
+        for _ in convolve(n, n, n == 1, late[n], 1 + n, [TAPS[0:8], TAPS[8:16], TAPS[16:18]], True):
             pass
-        into[late[n] : late[n] + 2] = convolved()
+        into[late[n] : late[n] + 2] = convolved(1 + n)
     v = pre[...]
     s = jax.nn.sigmoid(v)
     ext2[0, 2:6, own] = v * s
     ext2[1, 0:4, own] = d_active[...] * s * (1.0 + v * (1.0 - s))
-    swap = to_partner(ext2)
+    swap, swap2 = ((ext2.at[0, 0:4, 0:2], group()) for _ in range(2))
+    for n, frames, copies in ((1 - core, pl.ds(2 * core, 4), swap), (core, pl.ds(2 - 2 * core, 4), swap2)):
+        put(ext2.at[n, frames, own], ext2.at[n, frames, own], partner, copies[1])
+    to_leave += [swap, swap2]
 
     arrived(*passed)
 
@@ -408,6 +418,8 @@
     def finish():
         for n, out in ((0, block_ref), (1, gclip_ref)):
             near2, far2 = halo2
+            if n == 0:
+                arrived(*swap2)
             arrived(*near2[n])
             near_columns(ext2, n, own_of[n])
             yield
@@ -430,7 +442,7 @@
     order.sort()
     for at_event, (time, n) in enumerate(order):
         if time > 9.0 and not halo2:
-            halo2 += to_others(ext2)
+            halo2 += to_others(ext2, lambda n, frames, at_rows: ext2.at[n, frames, at_rows])
         next(running[n], None)
         if time > 14.0 and at_event + 1 < len(order):
             for _ in range(int((order[at_event + 1][0] - time) / 0.25)):
@@ -473,7 +485,7 @@
             pltpu.VMEM((2, 6, 6, 32, 128), F32),
             pltpu.VMEM((2, 6, 6, 32, 128), F32),
             pltpu.VMEM((2, 2, 3, 6, 6, 32, 128), BF16),
-            pltpu.VMEM((256, 256), F32),
+            pltpu.VMEM((3, 256, 256), F32),
             pltpu.VMEM((4, 2, 32, 128), F32),
             pltpu.VMEM((4, 2, 32, 128), F32),
             pltpu.VMEM((256, 512), BF16),

time: 61.8 us -> 61.6 us (level)
  no operation moved by 1% of the time
where the time goes in v6:
time: 61.6 us; the launch traced here: 61.5 us
  Pallas kernels  60.9 us (99%)
  between operations  0.64 us (1%)
    pallas_call x1, Pallas kernels, per_device(): pl.pallas_call(kernel, out_shape=(field, field, jax.ShapeDtypeStruct((2,...  59 us
    pallas_call x1, Pallas kernels, per_device(): pl.pallas_call(copy_out, out_shape=(field, field, grad, grad), in_specs=[...  1.94 us

profile of v6, /device:TPU:1, one launch (start us, length us, event | category | flops | bytes accessed | tf_op | source)
XLA Modules:
  0.0 61.5 jit_solution(7833904587005579443)
XLA Ops:
  0.6 59.0 %shard_map.75 = (f32[4,2,32,128]{3,2,1,0:T(8,128)S(1)}, f32[4,2,32,128]{3,2,1,0:T(8,128)S(1)}, f32[2,27,16,8,128]{4,3,2,1,0:T(8,128)S(1)}) custom-call(f32[4,2,32,128]{3,2,1,0:T(8,128)} %clip_ref.1, f32[4,2,32,128]{3,2,1,0:T(8,128)} %cot_ref.1, f32[27,128,128]{2,1,0:T(8,128)} %bitcast.4, f32[27,128,128]{2,1,0:T(8,128)} %bitcast.5), custom_call_target="tpu_custom_call" | custom-call | flops 5435817984 | bytes 8388608 | tf_op jit(solution)/shard_map/pallas_call | solution.py:476
  59.6 1.9 %shard_map.76 = (f32[4,2,32,128]{3,2,1,0:T(8,128)}, f32[4,2,32,128]{3,2,1,0:T(8,128)}, f32[27,16,8,128]{3,2,1,0:T(8,128)}, f32[27,16,8,128]{3,2,1,0:T(8,128)}) custom-call(f32[4,2,32,128]{3,2,1,0:T(8,128)S(1)} %get-tuple-element.11.block_ref, f32[4,2,32,128]{3,2,1,0:T(8,128)S(1)} %get-tuple-element.12.gclip_ref, ...), custom_call_target="tpu_custom_call" | custom-call | bytes 8388608 | tf_op jit(solution)/shard_map/pallas_call | solution.py:508

commit v7 on v6

--- a/solution.py
+++ b/solution.py
@@ -34,6 +34,7 @@
 
 plan()
 SEMAPHORES = (23, 65)
+FAR_FIRST = (4, 3, 5, 2, 6, 1, 7)
 Q = 1.0 / 256.0
 
 
@@ -71,12 +72,12 @@
         loads.append(pltpu.make_async_copy(src, dst, load_sem.at[len(loads)]))
         loads[-1].start()
 
-    peers = [partner, (tm, outer_row)]
+    plane = sorted(((d % 4, d // 4) for d in range(1, 16)), key=lambda to: -sum(min(d, 4 - d) for d in to))
+    peers = [at(x, y, lax.rem(z + d, 8)) for d in FAR_FIRST]
+    peers += [at(x + dx, y + dy, z) for dx, dy in plane]
     for t in (tm_next, tm_prev):
-        peers += [(t, rows), (t, partner_row), (t, outer_row)]
-    plane = [(d % 4, d // 4) for d in range(1, 16)]
-    peers += [at(x + dx, y + dy, z) for dx, dy in plane]
-    peers += [at(x, y, lax.rem(z + d, 8)) for d in range(1, 8)]
+        peers += [(t, outer_row), (t, partner_row), (t, rows)]
+    peers += [(tm, outer_row), partner]
     barrier = pltpu.get_barrier_semaphore()
     for peer in peers:
         pl.semaphore_signal(barrier, inc=1, device_id=peer, device_id_type=MESH)
@@ -136,12 +137,12 @@
             return ref.at[frames]
         return ref.at[frames, core if at_rows is edge else 1 - core]
 
-    near, far = to_others(ext, operand)
     beside = (ext.at[:, 0:4, 0:2], group())
     for n, mine, _, _, _ in sides:
         put(operand(n, mine, own), ext.at[n, mine, own], partner, beside[1])
     to_leave.append(beside)
 
+    near, far = to_others(ext, operand)
     for load in loads[:2]:
         load.wait()
     for load in loads[2:]:
@@ -284,19 +285,19 @@
             gradient(tap)
         yield
         sems = (ring_sends, new(1))
-        for d in (1, 2, 3):
+        for d in (2, 1, 3):
             put(part.at[taps, pl.ds(4 * p_of[d], 4)], r1.at[d - 1, taps], ring[d - 1], sems)
         yield
         arrived(r1.at[:, taps], sems)
         part[taps, pl.ds(4 * p, 4)] += r1[0, taps] + r1[1, taps] + r1[2, taps]
         sems = (ring2_sends, new(1))
-        for d in (1, 2, 3):
+        for d in (2, 1, 3):
             put(part.at[taps, 4 * p + s_of[d]], r2.at[d - 1, taps], ring2[d - 1], sems)
         yield
         arrived(r2.at[:, taps], sems)
         part[taps, tile] += r2[0, taps] + r2[1, taps] + r2[2, taps]
         sems = (z_sends, new(1))
-        for d in range(1, 8):
+        for d in FAR_FIRST:
             put(part.at[tap_at[d], tile], rz.at[which, d - 1], at(x, y, z_of[d]), sems, owns[d])
         yield
 
@@ -310,7 +311,7 @@
 
         done = mine.at[tap_at[0], tile]
         sems = (back_z, new(1))
-        for d in range(1, 8):
+        for d in FAR_FIRST:
             put(done, done, at(x, y, z_of[d]), sems, owns[0])
         yield
 
@@ -323,13 +324,13 @@
             arrived(mine.at[taps, tile], sems)
 
         sems = (back_ring2, new(1))
-        for to in ring2:
+        for to in (ring2[1], ring2[0], ring2[2]):
             same(mine.at[taps, tile], to, sems)
         yield
         arrived(r2.at[:, taps], sems)
         sems = (back_ring, new(1))
         chunks = [mine.at[taps, pl.ds(4 * i, 4)] for i in p_of]
-        for to in ring:
+        for to in (ring[1], ring[0], ring[2]):
             same(chunks[0], to, sems)
         same(chunks[0], partner, across)
         yield
@@ -371,7 +372,7 @@
         yield
         sems = group()
         to_leave.append((c1.at[:, got], sems))
-        for d in range(1, 8):
+        for d in FAR_FIRST:
             put(part.at[taps, pl.ds(2 * z_of[d], 2)], c1.at[d - 1, got], at(x, y, z_of[d]), sems)
         yield
         arrived(c1.at[:, got], sems)
@@ -404,7 +405,7 @@
         done = mine.at[taps, pl.ds(2 * z, 2)]
         sems = group()
         to_leave.append((c1.at[:, got], sems))
-        for d in range(1, 8):
+        for d in FAR_FIRST:
             same(done, at(x, y, z_of[d]), sems)
         same(done, partner, across)
         yield

time: 61.6 us -> 60.4 us (0.981)
  Pallas kernels: 60.9 us -> 59.7 us
    pallas_call x1, Pallas kernels: 59 us -> 57.8 us  [per_device(): pl.pallas_call(kernel, out_shape=(field, field, jax.ShapeDtypeStruct((2,...]
where the time goes in v7:
time: 60.4 us
  Pallas kernels  59.7 us (99%)
  between operations  0.64 us (1%)
    pallas_call x1, Pallas kernels, per_device(): pl.pallas_call(kernel, out_shape=(field, field, jax.ShapeDtypeStruct((2,...  57.8 us
    pallas_call x1, Pallas kernels, per_device(): pl.pallas_call(copy_out, out_shape=(field, field, grad, grad), in_specs=[...  1.94 us

profile of v7, /device:TPU:1, one launch (start us, length us, event | category | flops | bytes accessed | tf_op | source)
XLA Modules:
  0.0 60.4 jit_solution(3542897409408306238)
XLA Ops:
  0.6 57.8 %shard_map.75 = (f32[4,2,32,128]{3,2,1,0:T(8,128)S(1)}, f32[4,2,32,128]{3,2,1,0:T(8,128)S(1)}, f32[2,27,16,8,128]{4,3,2,1,0:T(8,128)S(1)}) custom-call(f32[4,2,32,128]{3,2,1,0:T(8,128)} %clip_ref.1, f32[4,2,32,128]{3,2,1,0:T(8,128)} %cot_ref.1, f32[27,128,128]{2,1,0:T(8,128)} %bitcast.4, f32[27,128,128]{2,1,0:T(8,128)} %bitcast.5), custom_call_target="tpu_custom_call" | custom-call | flops 5435817984 | bytes 8388608 | tf_op jit(solution)/shard_map/pallas_call | solution.py:477
  58.4 1.9 %shard_map.76 = (f32[4,2,32,128]{3,2,1,0:T(8,128)}, f32[4,2,32,128]{3,2,1,0:T(8,128)}, f32[27,16,8,128]{3,2,1,0:T(8,128)}, f32[27,16,8,128]{3,2,1,0:T(8,128)}) custom-call(f32[4,2,32,128]{3,2,1,0:T(8,128)S(1)} %get-tuple-element.11.block_ref, f32[4,2,32,128]{3,2,1,0:T(8,128)S(1)} %get-tuple-element.12.gclip_ref, ...), custom_call_target="tpu_custom_call" | custom-call | bytes 8388608 | tf_op jit(solution)/shard_map/pallas_call | solution.py:509

commit v8 on v7

--- a/solution.py
+++ b/solution.py
@@ -330,9 +330,9 @@
         arrived(r2.at[:, taps], sems)
         sems = (back_ring, new(1))
         chunks = [mine.at[taps, pl.ds(4 * i, 4)] for i in p_of]
+        same(chunks[0], partner, across)
         for to in (ring[1], ring[0], ring[2]):
             same(chunks[0], to, sems)
-        same(chunks[0], partner, across)
         yield
         arrived(r1.at[:, taps], sems)
         for chunk in chunks[1:]:
@@ -405,9 +405,9 @@
         done = mine.at[taps, pl.ds(2 * z, 2)]
         sems = group()
         to_leave.append((c1.at[:, got], sems))
+        same(done, partner, across)
         for d in FAR_FIRST:
             same(done, at(x, y, z_of[d]), sems)
-        same(done, partner, across)
         yield
         arrived(c1.at[:, got], sems)
         for d in range(1, 8):

time: 60.4 us -> 60.4 us (level)
  no operation moved by 1% of the time
where the time goes in v8:
time: 60.4 us
  Pallas kernels  59.7 us (99%)
  between operations  0.64 us (1%)
    pallas_call x1, Pallas kernels, per_device(): pl.pallas_call(kernel, out_shape=(field, field, jax.ShapeDtypeStruct((2,...  57.8 us
    pallas_call x1, Pallas kernels, per_device(): pl.pallas_call(copy_out, out_shape=(field, field, grad, grad), in_specs=[...  1.94 us

profile of v8, /device:TPU:1, one launch (start us, length us, event | category | flops | bytes accessed | tf_op | source)
XLA Modules:
  0.0 60.4 jit_solution(12149403204703261842)
XLA Ops:
  0.6 57.8 %shard_map.75 = (f32[4,2,32,128]{3,2,1,0:T(8,128)S(1)}, f32[4,2,32,128]{3,2,1,0:T(8,128)S(1)}, f32[2,27,16,8,128]{4,3,2,1,0:T(8,128)S(1)}) custom-call(f32[4,2,32,128]{3,2,1,0:T(8,128)} %clip_ref.1, f32[4,2,32,128]{3,2,1,0:T(8,128)} %cot_ref.1, f32[27,128,128]{2,1,0:T(8,128)} %bitcast.4, f32[27,128,128]{2,1,0:T(8,128)} %bitcast.5), custom_call_target="tpu_custom_call" | custom-call | flops 5435817984 | bytes 8388608 | tf_op jit(solution)/shard_map/pallas_call | solution.py:477
  58.4 1.9 %shard_map.76 = (f32[4,2,32,128]{3,2,1,0:T(8,128)}, f32[4,2,32,128]{3,2,1,0:T(8,128)}, f32[27,16,8,128]{3,2,1,0:T(8,128)}, f32[27,16,8,128]{3,2,1,0:T(8,128)}) custom-call(f32[4,2,32,128]{3,2,1,0:T(8,128)S(1)} %get-tuple-element.11.block_ref, f32[4,2,32,128]{3,2,1,0:T(8,128)S(1)} %get-tuple-element.12.gclip_ref, ...), custom_call_target="tpu_custom_call" | custom-call | bytes 8388608 | tf_op jit(solution)/shard_map/pallas_call | solution.py:509
